TPU v7x, 512 devices: a whole 4x4x16 slice. The times are simulated.
512 devices in a mesh: ctx: 64 (over z_lo, x, core), grp: 8 (over z_hi, y).
Axes of the slice: x: 4, y: 4, z: 16 (z_hi: 2, z_lo: 8; z = z_hi * 8 + z_lo), core: 2. Of those that a mesh axis runs over, the one named last changes fastest.
Arguments:
- queries: bfloat16 [8192, 4096], P('ctx', 'grp'), may hold values from -160 to 160
- key_vectors: bfloat16 [8192, 1024], P('ctx', 'grp'), may hold values from -6 to 6
- value_vectors: bfloat16 [8192, 1024], P('ctx', 'grp'), may hold values from -6 to 6
- grad_attn: bfloat16 [8192, 4096], P('ctx', 'grp'), may hold values from -6 to 6
- mamba_input: bfloat16 [8192, 16384], P('ctx', 'grp'), may hold values from -6 to 6
- step_sizes: bfloat16 [8192, 16384], P('ctx', 'grp'), may hold values from 0.0099487305 to 1
- decay_rates: float32 [16, 16384], P(None, 'grp'), may hold values from 0.0001 to 0.5
- write_coef: float32 [8192, 16], P('ctx'), may hold values from -1.5 to 1.5
- read_coef: float32 [8192, 16], P('ctx'), may hold values from -1.5 to 1.5
- grad_mamba: bfloat16 [8192, 16384], P('ctx', 'grp'), may hold values from -0.59765625 to 0.59765625
Outputs:
- grad_queries: bfloat16 [8192, 4096], P('ctx', 'grp')
- grad_keys: bfloat16 [8192, 1024], P('ctx', 'grp')
- grad_values: bfloat16 [8192, 1024], P('ctx', 'grp')
- grad_input: bfloat16 [8192, 16384], P('ctx', 'grp')
- grad_steps: bfloat16 [8192, 16384], P('ctx', 'grp')
- grad_write: float32 [8192, 16], P('ctx')
- grad_read: float32 [8192, 16], P('ctx')
All inputs are finite; a program needn't handle non-finite values.
Results may differ from a plain program's by a relative error of at most 0.008.
Values may be sent and summed in bfloat16 or wider, within the bound.
A program may use at most 128 MiB of HBM per device.

v0:
```python
import math

import jax
import jax.numpy as jnp
from jax import lax
from jax.sharding import PartitionSpec as P

HD = 128
QH_KV = 4
NST = 16


def carried_in(value, axis, combine, identity, reverse):
    peers, position = (lax.axis_size(axis), lax.axis_index(axis))
    everything = jax.tree.map(lambda part: lax.all_gather(part, axis), value)
    start = jax.tree.map(
        lambda part, zero: jnp.broadcast_to(jnp.asarray(zero, part.dtype), part.shape),
        value,
        identity,
    )

    def step(k, before):
        at = peers - 1 - k if reverse else k
        reached = at > position if reverse else at < position
        new = combine(before, jax.tree.map(lambda part: part[at], everything))
        return jax.tree.map(lambda a, b: jnp.where(reached, a, b), new, before)

    return lax.fori_loop(0, peers, step, start)


def chain_pair(earlier, later):
    return (earlier[0] * later[0], later[1] + later[0] * earlier[1])


def token_unit(tok_rows):
    return tok_rows // 16


def on_device(
    queries,
    key_vectors,
    value_vectors,
    grad_attn,
    mamba_input,
    step_sizes,
    decay_rates,
    write_coef,
    read_coef,
    grad_mamba,
):
    highest = lax.Precision.HIGHEST
    tok_rows = queries.shape[0]
    kv_local = key_vectors.shape[1] // HD
    score_scale = 1.0 / math.sqrt(HD)
    q_heads = queries.reshape(tok_rows, kv_local, QH_KV, HD)
    out_grad = grad_attn.reshape(tok_rows, kv_local, QH_KV, HD)
    all_keys, all_values = (
        lax.all_gather(key_vectors, "ctx", axis=0, tiled=True),
        lax.all_gather(value_vectors, "ctx", axis=0, tiled=True),
    )
    seq_rows = all_keys.shape[0]
    all_keys = all_keys.reshape(seq_rows, kv_local, HD)
    all_values = all_values.reshape(seq_rows, kv_local, HD)
    first_pos = lax.axis_index("ctx") * tok_rows
    query_pos = first_pos + jnp.arange(tok_rows, dtype=jnp.int32)
    key_block = math.gcd(seq_rows, 1024)
    needed = (first_pos + tok_rows - 1) // key_block + 1

    def block_scores(blk_index):
        blk_start = blk_index * key_block
        key_part = lax.dynamic_slice_in_dim(all_keys, blk_start, key_block, 0)
        value_part = lax.dynamic_slice_in_dim(all_values, blk_start, key_block, 0)
        scores = (
            jnp.einsum("tkgd,skd->kgts", q_heads, key_part, preferred_element_type=jnp.float32)
            * score_scale
        )
        visible = (blk_start + jnp.arange(key_block, dtype=jnp.int32))[None, :] <= query_pos[
            :, None
        ]
        return (scores, visible, key_part, value_part, blk_start)

    def forward_step(blk_index, carried):
        run_max, run_sum, run_acc = carried
        scores, visible, key_part, value_part, blk_start = block_scores(blk_index)
        scores = jnp.where(visible, scores, -jnp.inf)
        new_max = jnp.maximum(run_max, jnp.max(scores, axis=-1))
        prob_full = jnp.exp(scores - new_max[..., None])
        shrink = jnp.exp(run_max - new_max)
        run_acc = run_acc * shrink[..., None] + jnp.einsum(
            "kgts,skd->kgtd", prob_full, value_part.astype(jnp.float32), precision=highest
        )
        return (new_max, run_sum * shrink + jnp.sum(prob_full, axis=-1), run_acc)

    stat_shape = (kv_local, QH_KV, tok_rows)
    start_state = (
        jnp.full(stat_shape, -jnp.inf, jnp.float32),
        jnp.zeros(stat_shape, jnp.float32),
        jnp.zeros(stat_shape + (HD,), jnp.float32),
    )
    run_max, run_sum, run_acc = lax.fori_loop(0, needed, forward_step, start_state)
    log_total = run_max + jnp.log(run_sum)
    attn_out = run_acc / run_sum[..., None]
    row_dot = jnp.einsum(
        "tkgd,kgtd->kgt", out_grad.astype(jnp.float32), attn_out, precision=highest
    )

    def block_grads(blk_index):
        scores, visible, key_part, value_part, blk_start = block_scores(blk_index)
        prob_full = jnp.where(visible, jnp.exp(scores - log_total[..., None]), 0.0)
        weights = prob_full.astype(jnp.bfloat16)
        prob_grad = jnp.einsum(
            "tkgd,skd->kgts", out_grad, value_part, preferred_element_type=jnp.float32
        )
        score_grad = (prob_full * (prob_grad - row_dot[..., None]) * score_scale).astype(
            jnp.bfloat16
        )
        query_part = jnp.einsum(
            "kgts,skd->tkgd", score_grad, key_part, preferred_element_type=jnp.float32
        )
        return (query_part, score_grad, weights, blk_start)

    query_zero = jnp.zeros((tok_rows, kv_local, QH_KV, HD), jnp.float32)

    def backward_step(blk_index, carried):
        query_acc, term_rows = carried
        query_part, score_grad, weights, blk_start = block_grads(blk_index)
        key_term = jnp.einsum(
            "kgts,tkgd->skd", score_grad, q_heads, preferred_element_type=jnp.float32
        )
        value_term = jnp.einsum(
            "kgts,tkgd->skd", weights, out_grad, preferred_element_type=jnp.float32
        )
        term_rows = lax.dynamic_update_slice_in_dim(
            term_rows, jnp.concatenate([key_term, value_term], axis=-1), blk_start, 0
        )
        return (query_acc + query_part, term_rows)

    term_zero = jnp.zeros((seq_rows, kv_local, 2 * HD), jnp.float32)
    query_acc, term_rows = lax.fori_loop(0, needed, backward_step, (query_zero, term_zero))
    ctx_size = lax.axis_size("ctx")
    received = lax.all_to_all(
        term_rows.reshape(ctx_size, tok_rows, kv_local * 2 * HD),
        "ctx",
        split_axis=0,
        concat_axis=0,
        tiled=True,
    )
    summed = jnp.sum(received, axis=0).reshape(tok_rows, kv_local, 2 * HD)
    key_grad = summed[:, :, :HD]
    value_grad = summed[:, :, HD:]
    grad_queries = query_acc.astype(jnp.bfloat16).reshape(tok_rows, kv_local * QH_KV * HD)
    grad_keys = key_grad.astype(jnp.bfloat16).reshape(tok_rows, kv_local * HD)
    grad_values = value_grad.astype(jnp.bfloat16).reshape(tok_rows, kv_local * HD)
    channels = mamba_input.shape[1]
    unit = token_unit(tok_rows)
    blocks_n = tok_rows // unit

    def blocked(values):
        return values.reshape((blocks_n, unit) + values.shape[1:])

    x_blocks = blocked(mamba_input)
    step_blocks = blocked(step_sizes)
    gy_blocks = blocked(grad_mamba)
    write_blocks = blocked(write_coef)
    read_blocks = blocked(read_coef)

    def advance(state_now, x_tok, step_tok, write_tok):
        step_f = step_tok.astype(jnp.float32)
        decay_now = jnp.exp(-decay_rates * step_f[None, :])
        return (
            decay_now * state_now
            + (step_f * x_tok.astype(jnp.float32))[None, :] * write_tok[:, None],
            decay_now,
        )

    def forward_blocks(state_init):

        def outer(state_now, packed):
            x_block, step_block, write_block = packed
            block_start = state_now
            for offset in range(unit):
                state_now, decay_now = advance(
                    state_now, x_block[offset], step_block[offset], write_block[offset]
                )
            return (state_now, block_start)

        return lax.scan(outer, state_init, (x_blocks, step_blocks, write_blocks))

    step_total = jnp.sum(step_sizes.astype(jnp.float32), axis=0)
    zero_state = jnp.zeros((NST, channels), jnp.float32)
    end_local, unused = forward_blocks(zero_state)

    def backward_zero(carried, packed):
        step_block, read_block, gy_block = packed
        for offset in range(unit - 1, -1, -1):
            decay_now = jnp.exp(-decay_rates * step_block[offset].astype(jnp.float32)[None, :])
            grad_now = (
                read_block[offset][:, None] * gy_block[offset].astype(jnp.float32)[None, :]
                + carried
            )
            carried = decay_now * grad_now
        return (carried, None)

    grad_local, unused = lax.scan(
        backward_zero, zero_state, (step_blocks, read_blocks, gy_blocks), reverse=True
    )
    decay_total = jnp.exp(-decay_rates * step_total[None, :])
    identity = (jnp.ones_like(zero_state), zero_state)
    unused_decay, state_in = carried_in(
        (decay_total, end_local), "ctx", chain_pair, identity, False
    )
    unused_grad, grad_in = carried_in((decay_total, grad_local), "ctx", chain_pair, identity, True)
    unused_end, starts = forward_blocks(state_in)

    def backward_full(carried, packed):
        block_start, x_block, step_block, write_block, read_block, gy_block = packed
        states = []
        decays = []
        state_now = block_start
        for offset in range(unit):
            state_now, decay_now = advance(
                state_now, x_block[offset], step_block[offset], write_block[offset]
            )
            states.append(state_now)
            decays.append(decay_now)
        out_list = [None] * unit
        for offset in range(unit - 1, -1, -1):
            prev_state = states[offset - 1] if offset > 0 else block_start
            x_f = x_block[offset].astype(jnp.float32)
            step_f = step_block[offset].astype(jnp.float32)
            gy_f = gy_block[offset].astype(jnp.float32)
            write_tok = write_block[offset]
            grad_now = read_block[offset][:, None] * gy_f[None, :] + carried
            grad_x = jnp.sum(grad_now * write_tok[:, None], axis=0) * step_f
            grad_d = jnp.sum(
                grad_now
                * (write_tok[:, None] * x_f[None, :] - decay_rates * decays[offset] * prev_state),
                axis=0,
            )
            grad_w = jnp.sum(grad_now * (step_f * x_f)[None, :], axis=1)
            grad_r = jnp.sum(states[offset] * gy_f[None, :], axis=1)
            out_list[offset] = (grad_x, grad_d, grad_w, grad_r)
            carried = decays[offset] * grad_now
        stacked = jax.tree.map(lambda *parts: jnp.stack(parts), *out_list)
        return (carried, stacked)

    unused_carry, (grad_x, grad_d, grad_w, grad_r) = lax.scan(
        backward_full,
        grad_in,
        (starts, x_blocks, step_blocks, write_blocks, read_blocks, gy_blocks),
        reverse=True,
    )
    grad_input = grad_x.reshape(tok_rows, channels).astype(jnp.bfloat16)
    grad_steps = grad_d.reshape(tok_rows, channels).astype(jnp.bfloat16)
    grad_write, grad_read = lax.psum(
        (grad_w.reshape(tok_rows, NST), grad_r.reshape(tok_rows, NST)), "grp"
    )
    return (grad_queries, grad_keys, grad_values, grad_input, grad_steps, grad_write, grad_read)


def solution(mesh):
    return jax.shard_map(
        on_device,
        mesh=mesh,
        in_specs=(
            P("ctx", "grp"),
            P("ctx", "grp"),
            P("ctx", "grp"),
            P("ctx", "grp"),
            P("ctx", "grp"),
            P("ctx", "grp"),
            P(None, "grp"),
            P("ctx", None),
            P("ctx", None),
            P("ctx", "grp"),
        ),
        out_specs=(
            P("ctx", "grp"),
            P("ctx", "grp"),
            P("ctx", "grp"),
            P("ctx", "grp"),
            P("ctx", "grp"),
            P("ctx", None),
            P("ctx", None),
        ),
        check_vma=False,
    )
```

profile of v0, /device:TPU:32, one launch (start us, length us, event | category | flops | bytes accessed | tf_op | source)
XLA Modules:
  0.0 1254.7 jit_solution(3422784820025662196)
XLA Ops:
  10.6 1.6 multiply_exponential_fusion.8
  12.2 27.3 %while.126 = (s32[]{:T(128)}, f32[16,2048]{1,0:T(8,128)S(1)}, bf16[16,8,2048]{2,1,0:T(8,128)(2,1)}, f32[16,2048]{1,0:T(8,128)S(1)}, f32[16,8,16]{2,1,0:T(8,128)S...) while((s32[]{:T(128)}, f32[16,2048]{1,0:T(8,128)S(1)}, ...), condition=%wide.region_9.10_spmd.clone, body=%wide.region_8.9_spmd.clone.sunk | while | flops 1114123 | bytes 723755 | solution.py:204
  17.2 1.9 dynamic-slice_convert_fusion.82
  21.1 1.4 dynamic-slice_convert_fusion.82
  40.9 28.4 %while.128 = (s32[]{:T(128)}, f32[16,2048]{1,0:T(8,128)S(1)}, bf16[16,8,2048]{2,1,0:T(8,128)(2,1)}, f32[16,2048]{1,0:T(8,128)S(1)}, bf16[16,8,2048]{2,1,0:T(8,12...) while((s32[]{:T(128)}, f32[16,2048]{1,0:T(8,128)S(1)}, ...), condition=%wide.region_13.14_spmd.clone, body=%wide.region_12.13_spmd.clone.sunk | while | flops 1130506 | bytes 920343 | solution.py:187
  42.7 1.6 dynamic-slice_convert_fusion.83
  57.0 1.4 dynamic-slice_convert_fusion.83
  70.5 64.4 %all-gather.9.cloned.1.call-done = bf16[8192,128]{1,0:T(8,128)(2,1)} async-done(((bf16[128,128]{1,0:T(8,128)(2,1)}), bf16[8192,128]{1,0:T(8,128)(2,1)}) %all-gather.9.cloned.1.call-update) | async-done | bytes 2097168 | tf_op jit(solution)/shard_map/all_gather | solution.py:58
  134.9 118.6 %all-gather.11.cloned.1.call-done = bf16[8192,128]{1,0:T(8,128)(2,1)} async-done(((bf16[128,128]{1,0:T(8,128)(2,1)}), bf16[8192,128]{1,0:T(8,128)(2,1)}) %all-gather.11.cloned.1.call-update) | async-done | bytes 2097168 | tf_op jit(solution)/shard_map/all_gather | solution.py:59
  253.5 9.7 while.124
  253.8 1.4 fusion.111
  255.5 2.8 fusion.114
  258.6 1.4 fusion.111
  260.4 2.8 fusion.114
  263.8 3.8 broadcast_in_dim.127.clone
  267.5 13.9 %while.125 = (s32[]{:T(128)}, f32[128,1,4,128]{0,3,2,1:T(8,128)S(1)}, f32[8192,1,256]{2,0,1:T(8,128)}, s32[]{:T(128)}, bf16[8192,1,128]{2,0,1:T(8,128)(2,1)}, /*...) while((s32[]{:T(128)}, ...), condition=%wide.region_5.6_spmd.clone, body=%wide.region_4.5_spmd.clone.sunk | while | flops 675742848 | bytes 18887900 | solution.py:139
  267.7 1.5 fusion.125
  269.2 1.4 fusion.126
  274.7 1.5 fusion.125
  276.2 1.4 fusion.126
  282.2 9.0 copy.77
  291.2 78.3 %all-to-all-start = ((f32[64,128,256]{1,2,0:T(8,128)}), f32[64,128,256]{1,2,0:T(8,128)}, u32[]{:S(2)}, u32[]{:S(2)}) async-start(f32[64,128,256]{1,2,0:T(8,128)} %copy.77), calls=%async_computation | async-start | bytes 16777216 | tf_op jit(solution)/shard_map/all_to_all | solution.py:141
  369.5 19.0 %all-gather.13.cloned.1.call-done = f32[1024,2048]{1,0:T(8,128)} async-done(((f32[16,2048]{1,0:T(8,128)}), f32[1024,2048]{1,0:T(8,128)}) %all-gather.13.cloned.1.call-update) | async-done | bytes 8388624 | tf_op jit(solution)/shard_map/all_gather | solution.py:15
  388.5 395.2 %all-gather.15.cloned.1.call-done = f32[1024,2048]{1,0:T(8,128)} async-done(((f32[16,2048]{1,0:T(8,128)}), f32[1024,2048]{1,0:T(8,128)}) %all-gather.15.cloned.1.call-update) | async-done | bytes 8388624 | tf_op jit(solution)/shard_map/all_gather | solution.py:15
  783.7 70.4 %while.127 = (s32[]{:T(128)}, f32[16,2048]{1,0:T(8,128)S(1)}, s32[]{:T(128)}, f32[64,16,2048]{2,1,0:T(8,128)}, f32[64,16,2048]{2,1,0:T(8,128)}, /*index=5*/s32[]{:T(128)}, s32[]{:T(128)}, s32[]{:T(128)}, s32[]{:T(128)}) while((s32[]{:T(128)}, f32[16,2048]{1,0:T(8,128)S(1)}, s32[]{:T(128)}, f32[64,16,2048]{2,1,0:T(8,128)}, ...), condition=%wide.region_11.12_spmd.clone, body=%wide.region_10.11_spmd.clone.sunk | while | flops 131080 | bytes 524459 | solution.py:28
  854.1 57.3 %all-gather.17.cloned.1.call-done = f32[1024,2048]{1,0:T(8,128)} async-done(((f32[16,2048]{1,0:T(8,128)}), f32[1024,2048]{1,0:T(8,128)}) %all-gather.17.cloned.1.call-update) | async-done | bytes 8388624 | tf_op jit(solution)/shard_map/all_gather | solution.py:15
  911.4 69.9 %while.129 = (s32[]{:T(128)}, f32[16,2048]{1,0:T(8,128)S(1)}, s32[]{:T(128)}, f32[64,16,2048]{2,1,0:T(8,128)}, f32[64,16,2048]{2,1,0:T(8,128)}, /*index=5*/s32[]{:T(128)}, s32[]{:T(128)}) while((s32[]{:T(128)}, f32[16,2048]{1,0:T(8,128)S(1)}, s32[]{:T(128)}, f32[64,16,2048]{2,1,0:T(8,128)}, f32[64,16,2048]{2,1,0:T(8,128)}, ...), condition=%wide.region_15.16_spmd.clone, body=%wide.region_14.15_spmd.clone.sunk | while | flops 131076 | bytes 524397 | solution.py:28
  981.3 38.5 %while.122 = (s32[]{:T(128)}, f32[16,2048]{1,0:T(8,128)S(1)}, f32[16,16,2048]{2,1,0:T(8,128)}, bf16[16,8,2048]{2,1,0:T(8,128)(2,1)}, f32[16,2048]{1,0:T(8,128)S(...) while((s32[]{:T(128)}, f32[16,2048]{1,0:T(8,128)S(1)}, ...), condition=%wide.region_17.18_spmd, body=%wide.region_16.17_spmd.sunk | while | flops 1097737 | bytes 1182489 | solution.py:187
  984.4 1.6 dynamic-slice_convert_fusion.78
  1019.9 145.1 %while.123 = (s32[]{:T(128)}, f32[16,2048]{1,0:T(8,128)S(1)}, bf16[16,8,2048]{2,1,0:T(8,128)(2,1)S(1)}, bf16[16,8,2048]{2,1,0:T(8,128)(2,1)S(1)}, f32[16,8,16]{2...) while((s32[]{:T(128)}, f32[16,2048]{1,0:T(8,128)S(1)}, ...), condition=%wide.region_51.52_spmd, body=%wide.region_18.51_spmd.sunk | while | flops 6258442 | bytes 5268601 | solution.py:247
  1023.8 1.5 multiply_reduce_fusion.38
  1025.3 1.4 multiply_reduce_fusion.39
  1032.8 1.5 multiply_reduce_fusion.38
  1034.3 1.4 multiply_reduce_fusion.39
  1041.8 1.5 multiply_reduce_fusion.38
  1043.4 1.4 multiply_reduce_fusion.39
  1051.1 1.5 multiply_reduce_fusion.38
  1052.6 1.4 multiply_reduce_fusion.39
  1060.1 1.5 multiply_reduce_fusion.38
  1061.7 1.4 multiply_reduce_fusion.39
  1069.2 1.5 multiply_reduce_fusion.38
  1070.7 1.4 multiply_reduce_fusion.39
  1078.3 1.5 multiply_reduce_fusion.38
  1079.9 1.4 multiply_reduce_fusion.39
  1087.4 1.5 multiply_reduce_fusion.38
  1089.0 1.4 multiply_reduce_fusion.39
  1096.5 1.5 multiply_reduce_fusion.38
  1098.0 1.4 multiply_reduce_fusion.39
  1105.5 1.5 multiply_reduce_fusion.38
  1107.1 1.4 multiply_reduce_fusion.39
  1114.5 1.5 multiply_reduce_fusion.38
  1116.1 1.4 multiply_reduce_fusion.39
  1123.6 1.5 multiply_reduce_fusion.38
  1125.1 1.4 multiply_reduce_fusion.39
  1132.6 1.5 multiply_reduce_fusion.38
  1134.2 1.4 multiply_reduce_fusion.39
  1141.7 1.5 multiply_reduce_fusion.38
  1143.2 1.4 multiply_reduce_fusion.39
  1150.8 1.5 multiply_reduce_fusion.38
  1152.4 1.4 multiply_reduce_fusion.39
  1159.9 1.5 multiply_reduce_fusion.38
  1161.4 1.4 multiply_reduce_fusion.39
  1165.1 76.5 %all-reduce = (f32[128,16]{1,0:T(8,128)S(1)}, f32[128,16]{1,0:T(8,128)S(1)}) all-reduce(f32[128,16]{1,0:T(8,128)S(1)} %bitcast.850, f32[128,16]{1,0:T(8,128)S(1)} %bitcast.851), channel_id=1, replica_groups=mesh['ctx'=64,'grp'=8] {'grp'}, use_global_device_ids=true, to_apply=%region_52.53 | all-reduce | flops 4096 | bytes 32768 | tf_op jit(solution)/shard_map/psum | solution.py:255
  1242.9 3.8 reduce_sum.525
  (1189 shorter events, 333.5 us)
Async XLA Ops:
  7.2 127.8 %all-gather.9.cloned.1.call-start = ((), (), s32[]{:S(2)}) async-start(), calls=%async_computation.1 | async-start | bytes 2129920 | tf_op jit(solution)/shard_map/all_gather | solution.py:58
  7.9 245.6 %all-gather.11.cloned.1.call-start = ((), (), s32[]{:S(2)}) async-start(), calls=%async_computation.2 | async-start | bytes 2129920 | tf_op jit(solution)/shard_map/all_gather | solution.py:59
  8.6 379.8 %all-gather.13.cloned.1.call-start = ((), (), s32[]{:S(2)}) async-start(), calls=%async_computation.3 | async-start | bytes 8519680 | tf_op jit(solution)/shard_map/all_gather | solution.py:15
  12.2 28.6 %copy-start.7 = (f32[128,16]{0,1:T(8,128)S(1)}, f32[128,16]{0,1:T(8,128)}, u32[]{:S(2)}) copy-start(f32[128,16]{0,1:T(8,128)} %param.33) | copy-start | bytes 24580
  39.5 0.7 copy-start.1
  40.2 743.5 %all-gather.15.cloned.1.call-start = ((), (), s32[]{:S(2)}) async-start(), calls=%async_computation.4 | async-start | bytes 8519680 | tf_op jit(solution)/shard_map/all_gather | solution.py:15
  40.8 870.6 %all-gather.17.cloned.1.call-start = ((), (), s32[]{:S(2)}) async-start(), calls=%async_computation.5 | async-start | bytes 8519680 | tf_op jit(solution)/shard_map/all_gather | solution.py:15
  40.9 29.1 %copy-start.5 = (bf16[128,512]{1,0:T(8,128)(2,1)S(1)}, bf16[128,512]{1,0:T(8,128)(2,1)}, u32[]{:S(2)}) copy-start(bf16[128,512]{1,0:T(8,128)(2,1)} %param.29) | copy-start | bytes 393220
  40.9 29.3 %copy-start.6 = (bf16[128,512]{1,0:T(8,128)(2,1)S(1)}, bf16[128,512]{1,0:T(8,128)(2,1)}, u32[]{:S(2)}) copy-start(bf16[128,512]{1,0:T(8,128)(2,1)} %param.26) | copy-start | bytes 393220
  69.3 0.7 copy-start.2
  291.2 951.7 %all-to-all-start = ((f32[64,128,256]{1,2,0:T(8,128)}), f32[64,128,256]{1,2,0:T(8,128)}, u32[]{:S(2)}, u32[]{:S(2)}) async-start(f32[64,128,256]{1,2,0:T(8,128)} %copy.77), calls=%async_computation | async-start | bytes 16777216 | tf_op jit(solution)/shard_map/all_to_all | solution.py:141
  981.3 38.6 %copy-start = (f32[16,2048]{1,0:T(8,128)S(1)}, f32[16,2048]{1,0:T(8,128)}, u32[]{:S(2)}) copy-start(f32[16,2048]{1,0:T(8,128)} %param.32) | copy-start | bytes 393220
  1165.1 81.7 %copy-start.3 = (bf16[16,8,2048]{2,1,0:T(8,128)(2,1)}, bf16[16,8,2048]{2,1,0:T(8,128)(2,1)S(1)}, u32[]{:S(2)}) copy-start(bf16[16,8,2048]{2,1,0:T(8,128)(2,1)S(1)} %get-tuple-element.902) | copy-start | bytes 1572868
  1165.1 81.7 %copy-start.4 = (bf16[16,8,2048]{2,1,0:T(8,128)(2,1)}, bf16[16,8,2048]{2,1,0:T(8,128)(2,1)S(1)}, u32[]{:S(2)}) copy-start(bf16[16,8,2048]{2,1,0:T(8,128)(2,1)S(1)} %get-tuple-element.903) | copy-start | bytes 1572868
Sparse Core Ops, SparseCore 0:
  10.2 124.7 all-gather.8
  137.1 116.3 all-gather.10
  256.3 132.2 all-gather.12
  391.1 392.5 all-gather.14
  785.7 125.6 all-gather.16
where the time goes:
time: 1270 us; the launch traced here: 1250 us
  waiting for transfers between devices  656 us (52%)
  other arithmetic  362 us (29%)
  starting transfers between devices  78.5 us (6%)
  blocking collectives  76.5 us (6%)
  local copies, waits for them, and re-layouts  38.5 us (3%)
  matrix products  18.7 us (1%)
  between operations  14.1 us (1%)
    all_gather x3, waiting for transfers between devices, carried_in(): everything = jax.tree.map(lambda part: lax.all_gather(part, axis), value)  472 us
    select_n x128, other arithmetic, step(): return jax.tree.map(lambda a, b: jnp.where(reached, a, b), new, before)  137 us
    all_gather x1, waiting for transfers between devices, on_device(): lax.all_gather(value_vectors, 'ctx', axis=0, tiled=True)  119 us
    all_to_all x1, starting transfers between devices, on_device(): lax.all_to_all(term_rows.reshape(ctx_size, tok_rows, kv_local * 2 * HD),...  78.3 us
    psum x1, blocking collectives, on_device(): lax.psum((grad_w.reshape(tok_rows, NST), grad_r.reshape(tok_rows, NST)),...  76.5 us
    all_gather x1, waiting for transfers between devices, on_device(): lax.all_gather(key_vectors, 'ctx', axis=0, tiled=True)  64.4 us
    reduce_sum x48, other arithmetic, backward_full(): jnp.sum(grad_now * (write_tok[:, None] * x_f[None, :] - decay_rates * dec...  50.5 us
    convert_element_type x32, other arithmetic, advance(): x_tok.astype(jnp.float32)  43.7 us
  transfers between devices with their start and end apart: 6, of which 5 were waited for; matrix products, arithmetic and copies ran while one was open for 33% of the time, Pallas kernels for 0%

commit v1 on v0

v1 whole, which is shorter than its diff:
```python
import math

import jax
import jax.numpy as jnp
from jax import lax
from jax.experimental import pallas as pl
from jax.experimental.pallas import tpu as pltpu
from jax.sharding import PartitionSpec as P

MESH = pl.DeviceIdType.MESH
F32 = jnp.float32
BF16 = jnp.bfloat16
HD = 128
NST = 16
TOK = 128
PLANE = 8
NZ = 8
LOG2E = 1.4426950408889634
LN2 = 0.6931471805599453
SCALE = 1.0 / math.sqrt(HD)
NEG = -1e30
CW = 512
ROWS = 512


def dot(a, b, dims):
    return lax.dot_general(a, b, (dims, ((), ())), preferred_element_type=F32)


def kernel(
    q_ref, k_ref, v_ref, do_ref, x_ref, st_ref, rate_ref, b_ref, c_ref, gy_ref,
    dq_ref, dk_ref, dv_ref, gx_ref, gs_ref, gw_ref, gr_ref,
    qg, dog, kvg, stf, uf, gyf, bb, cb, tmp, ratel,
    ebuf, erecv, zmsg_up, zmsg_dn, zrecv_up, zrecv_dn, pre_f, pre_b, sin_f, sin_b, cbuf, crecv,
    mst, lst, rst, stat, lse, rdt,
    dqt, dqs, dqr, own, sib_s, sib_r, zs, zr,
    hs, avs, sg, sq, s1, s2, wacc, racc, wred, yrecv, hsum, hrecv,
    q_ss, q_rs, do_ss, do_rs, kz_ss, kz_rs, ks_ss, ks_rs, loc,
    ea_ss, ea_rs, eu_ss, eu_rs, ed_ss, ed_rs, ec_ss, ec_rs,
    sx_ss, sx_rs, dq_ss, dq_rs, si_ss, si_rs, zz_ss, zz_rs, y_ss, y_rs, hh_ss, hh_rs,
):
    channels = x_ref.shape[1]
    n_chunks = channels // CW
    slice_w = channels // PLANE
    c = lax.axis_index("ctx")
    g = lax.axis_index("grp")
    z = c // PLANE
    p = c % PLANE
    xx = p // 2
    core = p % 2
    sib = c + 1 - 2 * core
    base = z * PLANE
    y = g % 4
    gz = g - y

    def plane_peer(k):
        return (p + k) % PLANE

    def plane_from(k):
        return (p + PLANE - k) % PLANE

    def rcopy(src, dst, ss, rs, dev):
        return pltpu.make_async_remote_copy(
            src_ref=src, dst_ref=dst, send_sem=ss, recv_sem=rs, device_id=dev, device_id_type=MESH
        )

    bar = pltpu.get_barrier_semaphore()

    def greet(dev):
        pl.semaphore_signal(bar, inc=1, device_id=dev, device_id_type=MESH)

    for k in range(1, PLANE):
        greet({"ctx": base + plane_peer(k)})
    for k in range(1, NZ):
        greet({"ctx": ((z + k) % NZ) * PLANE + p})
    for k in range(1, 4):
        greet({"grp": gz + (y + k) % 4})
    greet({"grp": (g + 4) % 8})

    stf[...] = st_ref[...].astype(F32)
    uf[...] = stf[...] * x_ref[...].astype(F32)
    gyf[...] = gy_ref[...].astype(F32)
    ratel[...] = rate_ref[...] * (-LOG2E)
    tmp[...] = jnp.zeros_like(tmp)
    tmp[:, 0:NST] = b_ref[...]
    tmp[:, NST:2 * NST] = c_ref[...]
    bct = tmp[...].T[0:2 * NST, :]

    def spread(i, _):
        turned = pltpu.roll(bct, (TOK - 8 * i) % TOK, 1)
        for j in range(8):
            at = pl.ds(pl.multiple_of((8 * i + j) * NST, NST), NST)
            bb[at, :] = jnp.broadcast_to(turned[0:NST, j:j + 1], (NST, TOK))
            cb[at, :] = jnp.broadcast_to(turned[NST:2 * NST, j:j + 1], (NST, TOK))
        return 0

    lax.fori_loop(0, TOK // 8, spread, 0)

    kvg[z, pl.ds(pl.multiple_of(core * TOK, TOK), TOK), 0:HD] = k_ref[...]
    kvg[z, pl.ds(pl.multiple_of(core * TOK, TOK), TOK), HD:2 * HD] = v_ref[...]

    pl.semaphore_wait(bar, PLANE - 1 + NZ - 1 + 3 + 1)

    def q_copy(k, whole, gathered, ss, rs):
        dst = plane_peer(k)
        cols = pl.ds(pl.multiple_of((dst % 2) * 2 * HD, 2 * HD), 2 * HD)
        rows = pl.ds(pl.multiple_of(p * TOK, TOK), TOK)
        return rcopy(
            whole.at[:, cols], gathered.at[rows, :], ss.at[k], rs.at[k], {"ctx": base + dst}
        )

    def kv_copy(s, slot, to_sibling):
        rows = pl.ds(pl.multiple_of(core * TOK, TOK), TOK)
        part = kvg.at[slot, rows, :]
        if to_sibling:
            return rcopy(part, part, ks_ss.at[s], ks_rs.at[s], {"ctx": sib})
        return rcopy(part, part, kz_ss.at[s], kz_rs.at[s + 1], {"ctx": c + PLANE})

    def kv_step(s):
        slot = z - s

        @pl.when(slot >= 0)
        def _():
            @pl.when(s > 0)
            def _():
                part = kvg.at[slot, pl.ds(pl.multiple_of(core * TOK, TOK), TOK), :]
                rcopy(part, part, kz_ss.at[s], kz_rs.at[s], {"ctx": sib}).wait_recv()

            @pl.when(z < NZ - 1)
            def _():
                kv_copy(s, slot, False).start()

            kv_copy(s, slot, True).start()

    def kv_sib_wait(s):
        part = kvg.at[z - s, pl.ds(pl.multiple_of((1 - core) * TOK, TOK), TOK), :]
        rcopy(part, part, ks_ss.at[s], ks_rs.at[s], {"ctx": sib}).wait_recv()

    kv_step(jnp.int32(0))
    for k in range(1, PLANE):
        q_copy(k, q_ref, qg, q_ss, q_rs).start()
    for k in range(1, PLANE):
        q_copy(k, do_ref, dog, do_ss, do_rs).start()
    my_cols = pl.ds(pl.multiple_of(core * 2 * HD, 2 * HD), 2 * HD)
    my_rows = pl.ds(pl.multiple_of(p * TOK, TOK), TOK)
    loc_q = pltpu.make_async_copy(q_ref.at[:, my_cols], qg.at[my_rows, :], loc.at[0])
    loc_do = pltpu.make_async_copy(do_ref.at[:, my_cols], dog.at[my_rows, :], loc.at[1])
    loc_q.start()
    loc_do.start()

    def first_chunk(ch, _):
        lanes = pl.ds(pl.multiple_of(ch * CW, CW), CW)
        rt = ratel[:, lanes]

        def body(i, carry):
            h, pr, gg = carry
            for j in range(8):
                t = 8 * i + j
                at = pl.ds(pl.multiple_of(t * NST, NST), NST)
                bt = jnp.tile(bb[at, :], (1, CW // 128))
                ct = jnp.tile(cb[at, :], (1, CW // 128))
                a = jnp.exp2(rt * stf[pl.ds(t, 1), lanes])
                h = a * h + uf[pl.ds(t, 1), lanes] * bt
                pr = a * pr
                gg = gg + pr * (gyf[pl.ds(t, 1), lanes] * ct)
            return (h, pr, gg)

        zero = jnp.zeros((NST, CW), F32)
        h, pr, gg = lax.fori_loop(0, TOK // 8, body, (zero, jnp.ones((NST, CW), F32), zero))
        total = jnp.sum(stf[:, lanes], axis=0, keepdims=True)
        for half in range(CW // slice_w):
            to = ch * (CW // slice_w) + half
            cut = slice(half * slice_w, (half + 1) * slice_w)
            ebuf[to, 0:NST, :] = h[:, cut]
            ebuf[to, NST:2 * NST, :] = gg[:, cut]
            ebuf[to, 2 * NST:2 * NST + 8, :] = jnp.broadcast_to(total[:, cut], (8, slice_w))
        kv_step(ch + 1)
        return 0

    lax.fori_loop(0, n_chunks, first_chunk, 0)

    def e_copy(k):
        dst = plane_peer(k)
        return rcopy(ebuf.at[dst], erecv.at[p], ea_ss.at[k], ea_rs.at[k], {"ctx": base + dst})

    for k in range(1, PLANE):
        e_copy(k).start()
    own_e = pltpu.make_async_copy(ebuf.at[p], erecv.at[p], loc.at[2])
    own_e.start()

    mst[...] = jnp.full(mst.shape, NEG, F32)
    lst[...] = jnp.zeros_like(lst)
    rst[...] = jnp.zeros_like(rst)

    def tile_of(ch):
        head = ch // 2
        rows = pl.ds(pl.multiple_of((ch % 2) * ROWS, ROWS), ROWS)
        cols = pl.ds(pl.multiple_of(head * HD, HD), HD)
        lanes = pl.ds(pl.multiple_of(ch * ROWS, ROWS), ROWS)
        return rows, cols, lanes

    def seen(ch):
        key = xx * 2 * TOK + lax.broadcasted_iota(jnp.int32, (2 * TOK, ROWS), 0)
        query = (ch % 2) * ROWS + lax.broadcasted_iota(jnp.int32, (2 * TOK, ROWS), 1)
        return key <= query

    def attn_first(slot, diagonal):
        def body(ch, _):
            rows, cols, lanes = tile_of(ch)
            sc = dot(kvg[slot, :, 0:HD], qg[rows, cols], ((1,), (1,))) * (SCALE * LOG2E)
            if diagonal:
                sc = jnp.where(seen(ch), sc, NEG)
            sc = sc.reshape(2 * TOK // 8, 8, ROWS)
            dp = dot(kvg[slot, :, HD:2 * HD], dog[rows, cols], ((1,), (1,)))
            dp = dp.reshape(2 * TOK // 8, 8, ROWS)
            m_old = mst[:, lanes]
            m_new = jnp.maximum(m_old, jnp.max(sc, axis=0))
            shrink = jnp.exp2(m_old - m_new)
            pr = jnp.exp2(sc - m_new[None])
            mst[:, lanes] = m_new
            lst[:, lanes] = lst[:, lanes] * shrink + jnp.sum(pr, axis=0)
            rst[:, lanes] = rst[:, lanes] * shrink + jnp.sum(pr * dp, axis=0)
            return 0

        lax.fori_loop(0, 2 * 1024 // ROWS, body, 0)

    for k in range(1, PLANE):
        q_copy(k, q_ref, qg, q_ss, q_rs).wait()
        q_copy(k, do_ref, dog, do_ss, do_rs).wait()
    loc_q.wait()
    loc_do.wait()
    kv_sib_wait(jnp.int32(0))
    attn_first(z, True)

    for k in range(1, PLANE):
        e_copy(k).wait()
    own_e.wait()
    mine = pl.ds(pl.multiple_of(p * slice_w, slice_w), slice_w)
    rslice = ratel[:, mine]
    zero_s = jnp.zeros((NST, slice_w), F32)
    state = zero_s
    total = jnp.zeros((1, slice_w), F32)
    for j in range(PLANE):
        pre_f[j, 0:NST, :] = state
        pre_f[j, NST:2 * NST, :] = jnp.exp2(rslice * total)
        tj = erecv[j, 2 * NST:2 * NST + 1, :]
        state = jnp.exp2(rslice * tj) * state + erecv[j, 0:NST, :]
        total = total + tj
    plane_total = total
    zmsg_up[0:NST, :] = state
    zmsg_up[NST:NST + 8, :] = jnp.broadcast_to(plane_total, (8, slice_w))
    state = zero_s
    total = jnp.zeros((1, slice_w), F32)
    for j in range(PLANE - 1, -1, -1):
        pre_b[j, 0:NST, :] = state
        pre_b[j, NST:2 * NST, :] = jnp.exp2(rslice * total)
        tj = erecv[j, 2 * NST:2 * NST + 1, :]
        state = jnp.exp2(rslice * tj) * state + erecv[j, NST:2 * NST, :]
        total = total + tj
    zmsg_dn[0:NST, :] = state
    zmsg_dn[NST:NST + 8, :] = jnp.broadcast_to(plane_total, (8, slice_w))

    def up_copy(k):
        return rcopy(
            zmsg_up, zrecv_up.at[k], eu_ss.at[k], eu_rs.at[k], {"ctx": c + k * PLANE}
        )

    def dn_copy(k):
        return rcopy(
            zmsg_dn, zrecv_dn.at[k], ed_ss.at[k], ed_rs.at[k], {"ctx": c - k * PLANE}
        )

    for k in range(1, NZ):
        @pl.when(z + k < NZ)
        def _(k=k):
            up_copy(k).start()

        @pl.when(z - k >= 0)
        def _(k=k):
            dn_copy(k).start()

    def attn_step(s, _):
        @pl.when(s > n_chunks)
        def _():
            kv_step(s)

        kv_sib_wait(s)
        attn_first(z - s, False)
        return 0

    lax.fori_loop(1, z + 1, attn_step, 0)

    m8 = mst[...]
    m1 = jnp.max(m8, axis=0, keepdims=True)
    w8 = jnp.exp2(m8 - m1)
    l1 = jnp.sum(lst[...] * w8, axis=0, keepdims=True)
    r1 = jnp.sum(rst[...] * w8, axis=0, keepdims=True)
    n_rt = 2 * 1024 // 128
    for j in range(n_rt):
        cut = slice(j * 128, (j + 1) * 128)
        stat[0, j:j + 1, :] = m1[:, cut]
        stat[0, n_rt + j:n_rt + j + 1, :] = l1[:, cut]
        stat[0, 2 * n_rt + j:2 * n_rt + j + 1, :] = r1[:, cut]

    def stat_copy(k):
        dst = base + ((xx + k) % 4) * 2 + core
        return rcopy(stat.at[0], stat.at[k], sx_ss.at[k], sx_rs.at[k], {"ctx": dst})

    for k in range(1, 4):
        stat_copy(k).start()

    sin_f[...] = zero_s
    sin_b[...] = zero_s
    for k in range(NZ - 1, 0, -1):
        @pl.when(z - k >= 0)
        def _(k=k):
            rcopy(
                zmsg_up, zrecv_up.at[k], eu_ss.at[k], eu_rs.at[k], {"ctx": sib}
            ).wait_recv()
            dec = jnp.exp2(rslice * zrecv_up[k, NST:NST + 1, :])
            sin_f[...] = dec * sin_f[...] + zrecv_up[k, 0:NST, :]

        @pl.when(z + k < NZ)
        def _(k=k):
            rcopy(
                zmsg_dn, zrecv_dn.at[k], ed_ss.at[k], ed_rs.at[k], {"ctx": sib}
            ).wait_recv()
            dec = jnp.exp2(rslice * zrecv_dn[k, NST:NST + 1, :])
            sin_b[...] = dec * sin_b[...] + zrecv_dn[k, 0:NST, :]
    for j in range(PLANE):
        cbuf[j, 0:NST, :] = pre_f[j, 0:NST, :] + pre_f[j, NST:2 * NST, :] * sin_f[...]
        cbuf[j, NST:2 * NST, :] = pre_b[j, 0:NST, :] + pre_b[j, NST:2 * NST, :] * sin_b[...]

    def c_copy(k):
        dst = plane_peer(k)
        return rcopy(cbuf.at[dst], crecv.at[p], ec_ss.at[k], ec_rs.at[k], {"ctx": base + dst})

    for k in range(1, PLANE):
        c_copy(k).start()
    own_c = pltpu.make_async_copy(cbuf.at[p], crecv.at[p], loc.at[3])
    own_c.start()

    for k in range(1, 4):
        stat_copy(k).wait()
    m4 = [stat[k, 0:n_rt, :] for k in range(4)]
    m_all = jnp.maximum(jnp.maximum(m4[0], m4[1]), jnp.maximum(m4[2], m4[3]))
    l_all = jnp.zeros((n_rt, 128), F32)
    r_all = jnp.zeros((n_rt, 128), F32)
    for k in range(4):
        w = jnp.exp2(m4[k] - m_all)
        l_all = l_all + w * stat[k, n_rt:2 * n_rt, :]
        r_all = r_all + w * stat[k, 2 * n_rt:3 * n_rt, :]
    lse_t = m_all + jnp.log2(l_all)
    rd_t = r_all / l_all
    for j in range(n_rt):
        cut = slice(j * 128, (j + 1) * 128)
        lse[:, cut] = jnp.broadcast_to(lse_t[j:j + 1, :], (8, 128))
        rdt[:, cut] = jnp.broadcast_to(rd_t[j:j + 1, :], (8, 128))

    dqt[...] = jnp.zeros_like(dqt)

    def attn_second(s, slot, diagonal):
        keys_t = kvg[slot, :, 0:HD].T

        def body(ch, carry):
            dk, dv = carry
            rows, cols, lanes = tile_of(ch)
            keys = kvg[slot, :, 0:HD]
            sc = dot(keys, qg[rows, cols], ((1,), (1,))) * (SCALE * LOG2E)
            pr = jnp.exp2(sc.reshape(2 * TOK // 8, 8, ROWS) - lse[:, lanes][None])
            if diagonal:
                pr = jnp.where(seen(ch).reshape(pr.shape), pr, 0.0)
            dp = dot(kvg[slot, :, HD:2 * HD], dog[rows, cols], ((1,), (1,)))
            ds = pr * (dp.reshape(pr.shape) - rdt[:, lanes][None])
            pb = pr.reshape(2 * TOK, ROWS).astype(BF16)
            db = ds.reshape(2 * TOK, ROWS).astype(BF16)
            dv = dv + dot(pb, dog[rows, cols], ((1,), (0,)))
            dk = dk + dot(db, qg[rows, cols], ((1,), (0,)))
            head = pl.ds(pl.multiple_of((ch // 2) * HD, HD), HD)
            dqt[head, rows] += dot(keys_t, db, ((1,), (0,)))
            return dk, dv

        zero = jnp.zeros((2 * TOK, HD), F32)
        dk, dv = lax.fori_loop(0, 2 * 1024 // ROWS, body, (zero, zero))
        dk = dk * SCALE
        first = core == 0
        own[s, :, 0:HD] = jnp.where(first, dk[0:TOK], dk[TOK:])
        own[s, :, HD:2 * HD] = jnp.where(first, dv[0:TOK], dv[TOK:])
        sib_s[s, :, 0:HD] = jnp.where(first, dk[TOK:], dk[0:TOK])
        sib_s[s, :, HD:2 * HD] = jnp.where(first, dv[TOK:], dv[0:TOK])
        sib_copy(s).start()

    def sib_copy(s):
        return rcopy(sib_s.at[s], sib_r.at[s], si_ss.at[s], si_rs.at[s], {"ctx": sib})

    def z_copy(s):
        return rcopy(
            zs.at[s], zr.at[s], zz_ss.at[s], zz_rs.at[s], {"ctx": c - s * PLANE}
        )

    def hand_down(s):
        sib_copy(s).wait()
        zs[s] = (own[s] + sib_r[s]).astype(BF16)
        z_copy(s).start()

    def second_step(i, _):
        s = z - i
        attn_second(s, z - s, False)

        @pl.when(i > 0)
        def _():
            hand_down(s + 1)

        return 0

    lax.fori_loop(0, z, second_step, 0)
    attn_second(jnp.int32(0), z, True)

    @pl.when(z > 0)
    def _():
        hand_down(jnp.int32(1))

    dqs[...] = (dqt[...] * SCALE).astype(BF16)

    def dq_copy(k):
        dst = plane_peer(k)
        cols = pl.ds(pl.multiple_of(dst * TOK, TOK), TOK)
        return rcopy(
            dqs.at[:, cols], dqr.at[p], dq_ss.at[k], dq_rs.at[k], {"ctx": base + dst}
        )

    for k in range(1, PLANE):
        dq_copy(k).start()
    own_dq = pltpu.make_async_copy(
        dqs.at[:, pl.ds(pl.multiple_of(p * TOK, TOK), TOK)], dqr.at[p], loc.at[4]
    )
    own_dq.start()
    sib_copy(jnp.int32(0)).wait()

    for k in range(1, PLANE):
        c_copy(k).wait()
    own_c.wait()

    def second_chunk(ch, _):
        lanes = pl.ds(pl.multiple_of(ch * CW, CW), CW)
        rt = ratel[:, lanes]
        per = CW // slice_w
        h_in = jnp.concatenate([crecv[ch * per + i, 0:NST, :] for i in range(per)], axis=1)
        g_in = jnp.concatenate([crecv[ch * per + i, NST:2 * NST, :] for i in range(per)], axis=1)
        hs[0:NST, :] = h_in

        def forward(i, h):
            for j in range(8):
                t = 8 * i + j
                at = pl.ds(pl.multiple_of(t * NST, NST), NST)
                bt = jnp.tile(bb[at, :], (1, CW // 128))
                a = jnp.exp2(rt * stf[pl.ds(t, 1), lanes])
                h = a * h + uf[pl.ds(t, 1), lanes] * bt
                avs[at, :] = a
                hs[pl.ds(pl.multiple_of((t + 1) * NST, NST), NST), :] = h
            return h

        lax.fori_loop(0, TOK // 8, forward, h_in)

        def folded(v):
            out = v[:, 0:128]
            for i in range(1, CW // 128):
                out = out + v[:, i * 128:(i + 1) * 128]
            return out

        def backward(i, carry):
            lo = TOK // 8 - 1 - i
            for j in range(7, -1, -1):
                t = 8 * lo + j
                at = pl.ds(pl.multiple_of(t * NST, NST), NST)
                bt = jnp.tile(bb[at, :], (1, CW // 128))
                ct = jnp.tile(cb[at, :], (1, CW // 128))
                gyt = gyf[pl.ds(t, 1), lanes]
                gn = ct * gyt + carry
                carry = avs[at, :] * gn
                qv = carry * rt * hs[at, :]
                gb = gn * bt
                for v in range(CW // 128):
                    cut = slice(v * 128, (v + 1) * 128)
                    sg[v, j * 8:(j + 1) * 8, :] = gb[0:8, cut] + gb[8:16, cut]
                    sq[v, j * 8:(j + 1) * 8, :] = qv[0:8, cut] + qv[8:16, cut]
                wacc[at, :] += folded(gn * uf[pl.ds(t, 1), lanes])
                racc[at, :] += folded(
                    hs[pl.ds(pl.multiple_of((t + 1) * NST, NST), NST), :] * gyt
                )
            rows = pl.ds(pl.multiple_of(8 * lo, 8), 8)
            for v in range(CW // 128):
                cut = slice(v * 128, (v + 1) * 128)
                a1 = sg[v, pl.ds(0, 8, stride=8), :]
                a2 = sq[v, pl.ds(0, 8, stride=8), :]
                for n in range(1, 8):
                    a1 = a1 + sg[v, pl.ds(n, 8, stride=8), :]
                    a2 = a2 + sq[v, pl.ds(n, 8, stride=8), :]
                s1[rows, cut] = a1
                s2[rows, cut] = a2
            return carry

        lax.fori_loop(0, TOK // 8, backward, g_in)
        gx_ref[:, lanes] = (s1[...] * stf[:, lanes]).astype(BF16)
        gs_ref[:, lanes] = (
            s1[...] * x_ref[:, lanes].astype(F32) + LN2 * s2[...]
        ).astype(BF16)
        return 0

    wacc[...] = jnp.zeros_like(wacc)
    racc[...] = jnp.zeros_like(racc)
    lax.fori_loop(0, n_chunks, second_chunk, 0)

    def lanes_sum(i, _):
        at = pl.ds(pl.multiple_of(i * 8 * NST, 8 * NST), 8 * NST)
        row = lax.broadcasted_iota(jnp.int32, (8 * NST, 128), 0) % NST
        lane = lax.broadcasted_iota(jnp.int32, (8 * NST, 128), 1)
        ws = jnp.sum(wacc[at, :], axis=1, keepdims=True)
        rs = jnp.sum(racc[at, :], axis=1, keepdims=True)
        both = jnp.where(lane == row, ws, 0.0) + jnp.where(lane == row + NST, rs, 0.0)
        tmp[pl.ds(pl.multiple_of(i * 8, 8), 8), :] = jnp.sum(both.reshape(8, NST, 128), axis=1)
        return 0

    lax.fori_loop(0, TOK // 8, lanes_sum, 0)
    wred[...] = tmp[...].T[0:2 * NST, :]

    def y_copy(k):
        return rcopy(wred, yrecv.at[k], y_ss.at[k], y_rs.at[k], {"grp": gz + (y + k) % 4})

    for k in range(1, 4):
        y_copy(k).start()

    for k in range(1, PLANE):
        dq_copy(k).wait()
    own_dq.wait()
    for cc in range(2):
        tot = dqr[cc].astype(F32)
        for i in range(1, 4):
            tot = tot + dqr[2 * i + cc].astype(F32)
        for h in range(2):
            col = (cc * 2 + h) * HD
            dq_ref[:, col:col + HD] = tot[h * HD:(h + 1) * HD, :].T.astype(BF16)

    for k in range(1, 4):
        y_copy(k).wait()
    hsum[...] = wred[...] + yrecv[1] + yrecv[2] + yrecv[3]
    h_copy = rcopy(hsum, hrecv, hh_ss, hh_rs, {"grp": (g + 4) % 8})
    h_copy.start()

    own[0] = own[0] + sib_r[0]
    for k in range(1, NZ):
        @pl.when(z + k < NZ)
        def _(k=k):
            rcopy(zs.at[k], zr.at[k], zz_ss.at[k], zz_rs.at[k], {"ctx": sib}).wait_recv()
            own[0] = own[0] + zr[k].astype(F32)
    dk_ref[...] = own[0, :, 0:HD].astype(BF16)
    dv_ref[...] = own[0, :, HD:2 * HD].astype(BF16)

    h_copy.wait()
    tmp[0:2 * NST, :] = hsum[...] + hrecv[...]
    back = tmp[...].T
    gw_ref[...] = back[:, 0:NST]
    gr_ref[...] = back[:, NST:2 * NST]

    for k in range(1, NZ):
        @pl.when(z + k < NZ)
        def _(k=k):
            up_copy(k).wait_send()

        @pl.when(z - k >= 0)
        def _(k=k):
            dn_copy(k).wait_send()
            z_copy(k).wait_send()
    for s in range(NZ):
        @pl.when(z - s >= 0)
        def _(s=s):
            kv_copy(s, z - s, True).wait_send()

            @pl.when(z < NZ - 1)
            def _():
                kv_copy(s, z - s, False).wait_send()


def on_device(
    queries, key_vectors, value_vectors, grad_attn, mamba_input, step_sizes, decay_rates,
    write_coef, read_coef, grad_mamba,
):
    channels = mamba_input.shape[1]
    slice_w = channels // PLANE
    vmem = pltpu.VMEM
    dma = pltpu.SemaphoreType.DMA
    scratch = [
        vmem((1024, 256), BF16), vmem((1024, 256), BF16), vmem((NZ, 256, 256), BF16),
        vmem((TOK, channels), F32), vmem((TOK, channels), F32), vmem((TOK, channels), F32),
        vmem((TOK * NST, 128), F32), vmem((TOK * NST, 128), F32), vmem((128, 128), F32),
        vmem((NST, channels), F32),
        vmem((PLANE, 40, slice_w), F32), vmem((PLANE, 40, slice_w), F32),
        vmem((24, slice_w), F32), vmem((24, slice_w), F32),
        vmem((NZ, 24, slice_w), F32), vmem((NZ, 24, slice_w), F32),
        vmem((PLANE, 32, slice_w), F32), vmem((PLANE, 32, slice_w), F32),
        vmem((NST, slice_w), F32), vmem((NST, slice_w), F32),
        vmem((PLANE, 32, slice_w), F32), vmem((PLANE, 32, slice_w), F32),
        vmem((8, 2048), F32), vmem((8, 2048), F32), vmem((8, 2048), F32),
        vmem((4, 48, 128), F32), vmem((8, 2048), F32), vmem((8, 2048), F32),
        vmem((256, 1024), F32), vmem((256, 1024), BF16), vmem((PLANE, 256, 128), BF16),
        vmem((NZ, 128, 256), F32), vmem((NZ, 128, 256), F32), vmem((NZ, 128, 256), F32),
        vmem((NZ, 128, 256), BF16), vmem((NZ, 128, 256), BF16),
        vmem(((TOK + 1) * NST, CW), F32), vmem((TOK * NST, CW), F32),
        vmem((CW // 128, 64, 128), F32), vmem((CW // 128, 64, 128), F32), vmem((TOK, CW), F32), vmem((TOK, CW), F32),
        vmem((TOK * NST, 128), F32), vmem((TOK * NST, 128), F32),
        vmem((32, 128), F32), vmem((4, 32, 128), F32), vmem((32, 128), F32), vmem((32, 128), F32),
        dma((8,)), dma((8,)), dma((8,)), dma((8,)), dma((8,)), dma((8,)), dma((8,)), dma((8,)),
        dma((8,)),
        dma((8,)), dma((8,)), dma((8,)), dma((8,)), dma((8,)), dma((8,)), dma((8,)), dma((8,)),
        dma((4,)), dma((4,)), dma((8,)), dma((8,)), dma((8,)), dma((8,)), dma((8,)), dma((8,)),
        dma((4,)), dma((4,)), dma, dma,
    ]
    outs = (
        jax.ShapeDtypeStruct(queries.shape, BF16),
        jax.ShapeDtypeStruct(key_vectors.shape, BF16),
        jax.ShapeDtypeStruct(value_vectors.shape, BF16),
        jax.ShapeDtypeStruct(mamba_input.shape, BF16),
        jax.ShapeDtypeStruct(step_sizes.shape, BF16),
        jax.ShapeDtypeStruct(write_coef.shape, F32),
        jax.ShapeDtypeStruct(read_coef.shape, F32),
    )
    return pl.pallas_call(
        kernel,
        out_shape=outs,
        in_specs=[pl.BlockSpec(memory_space=pltpu.VMEM)] * 10,
        out_specs=(pl.BlockSpec(memory_space=pltpu.VMEM),) * 7,
        scratch_shapes=scratch,
        compiler_params=pltpu.CompilerParams(
            collective_id=0, has_side_effects=True, vmem_limit_bytes=56 * 2**20
        ),
    )(
        queries, key_vectors, value_vectors, grad_attn, mamba_input, step_sizes, decay_rates,
        write_coef, read_coef, grad_mamba,
    )


def solution(mesh):
    both = P("ctx", "grp")
    rows = P("ctx", None)
    return jax.shard_map(
        on_device,
        mesh=mesh,
        in_specs=(both,) * 6 + (P(None, "grp"), rows, rows, both),
        out_specs=(both,) * 5 + (rows, rows),
        check_vma=False,
    )
```

time: 1270 us -> 110 us (0.09)
  the two profiles are of different devices: /device:TPU:32 before, /device:TPU:486 now
where the time goes in v1:
time: 110 us
  Pallas kernels  97.3 us (88%)
  local copies, waits for them, and re-layouts  11.6 us (11%)
    pallas_call x1, Pallas kernels, on_device(): pl.pallas_call(kernel, out_shape=outs, in_specs=[pl.BlockSpec(memory_spac...  97.3 us
    unnamed x13, local copies, waits for them, and re-layouts  8.51 us
    pallas_call x2, local copies, waits for them, and re-layouts, on_device(): pl.pallas_call(kernel, out_shape=outs, in_specs=[pl.BlockSpec(memory_spac...  3.07 us

profile of v1, /device:TPU:486, one launch (start us, length us, event | category | flops | bytes accessed | tf_op | source)
XLA Modules:
  0.0 109.5 jit_solution(15084268768784459952)
XLA Ops:
  0.6 0.0 copy-start.2
  0.6 1.4 %copy.17.b_ref = f32[128,16]{1,0:T(8,128)} copy(f32[128,16]{0,1:T(8,128)} %param.17) | data formatting | bytes 16384 | tf_op args[7]
  2.1 0.0 copy-done.2
  2.1 0.7 copy.18.c_ref
  2.8 97.3 %shard_map.153 = (bf16[128,512]{1,0:T(8,128)(2,1)}, bf16[128,128]{1,0:T(8,128)(2,1)}, bf16[128,128]{1,0:T(8,128)(2,1)}, bf16[128,2048]{1,0:T(8,128)(2,1)}, bf16[...) custom-call(bf16[128,512]{1,0:T(8,128)(2,1)} %q_ref.1, bf16[128,128]{1,0:T(8,128)(2,1)} %k_ref.1, ...), custom_call_target="tpu_custom_call" | custom-call | tf_op jit(solution)/shard_map/pallas_call | solution.py:627
  100.1 0.0 copy-start.1
  100.1 1.6 %copy.19 = f32[128,16]{0,1:T(8,128)} copy(f32[128,16]{1,0:T(8,128)} %get-tuple-element.12) | data formatting | bytes 16384 | tf_op jit(solution)/shard_map/pallas_call | solution.py:627
  101.7 1.5 %copy.20 = f32[128,16]{0,1:T(8,128)} copy(f32[128,16]{1,0:T(8,128)} %get-tuple-element.13) | data formatting | bytes 16384 | tf_op jit(solution)/shard_map/pallas_call | solution.py:627
  103.2 1.6 %copy.26 = bf16[128,512]{1,0:T(8,128)(2,1)} copy(bf16[128,512]{1,0:T(8,128)(2,1)} %get-tuple-element.21) | data formatting | bytes 262144
  104.8 1.4 %copy.27 = bf16[128,128]{1,0:T(8,128)(2,1)} copy(bf16[128,128]{1,0:T(8,128)(2,1)} %get-tuple-element.22) | data formatting | bytes 65536
  106.1 1.4 %copy.28 = bf16[128,128]{1,0:T(8,128)(2,1)} copy(bf16[128,128]{1,0:T(8,128)(2,1)} %get-tuple-element.23) | data formatting | bytes 65536
  107.5 0.0 copy-done.1
  107.5 0.0 copy-start
  107.5 0.8 copy.29
  108.3 0.4 copy-done
  108.7 0.8 copy.30
Async XLA Ops:
  0.6 1.4 %copy-start.2 = (f32[128,16]{0,1:T(8,128)S(1)}, f32[128,16]{0,1:T(8,128)}, u32[]{:S(2)}) copy-start(f32[128,16]{0,1:T(8,128)} %param.18) | copy-start | bytes 24580
  100.1 7.4 %copy-start.1 = (bf16[128,2048]{1,0:T(8,128)(2,1)S(1)}, bf16[128,2048]{1,0:T(8,128)(2,1)}, u32[]{:S(2)}) copy-start(bf16[128,2048]{1,0:T(8,128)(2,1)} %get-tuple-element.24) | copy-start | bytes 1572868
  107.5 1.2 %copy-start = (bf16[128,2048]{1,0:T(8,128)(2,1)S(1)}, bf16[128,2048]{1,0:T(8,128)(2,1)}, u32[]{:S(2)}) copy-start(bf16[128,2048]{1,0:T(8,128)(2,1)} %get-tuple-element.25) | copy-start | bytes 1572868

commit v2 on v1

v2 whole, which is shorter than its diff:
```python
import math

import jax
import jax.numpy as jnp
from jax import lax
from jax.experimental import pallas as pl
from jax.experimental.pallas import tpu as pltpu
from jax.sharding import PartitionSpec as P

MESH = pl.DeviceIdType.MESH
F32 = jnp.float32
BF16 = jnp.bfloat16
HD = 128
NST = 16
TOK = 128
PLANE = 8
NZ = 8
LOG2E = 1.4426950408889634
LN2 = 0.6931471805599453
SCALE = 1.0 / math.sqrt(HD)
NEG = -1e30
CW = 512
ROWS = 512
KV_ROWS = 32


def dot(a, b, dims):
    return lax.dot_general(a, b, (dims, ((), ())), preferred_element_type=F32)


def kernel(
    q_ref, k_ref, v_ref, do_ref, x_ref, st_ref, rate_ref, b_ref, c_ref, gy_ref,
    dq_ref, dk_ref, dv_ref, gx_ref, gs_ref, gw_ref, gr_ref,
    xb, stb, gyb, rates, bct, spr, qg, dog, kvg, stf, uf, gyf, bb, cb, tmp, ratel,
    ebuf, erecv, zmsg_up, zmsg_dn, zrecv_up, zrecv_dn, pre_f, pre_b, sin_f, sin_b, cbuf, crecv,
    mst, lst, rst, stat, lse, rdt,
    dqt, dqs, dqr, own, sib_s, sib_r, zs, zr,
    hs, avs, cum, sg, sq, s1, s2, wacc, racc, wred, yrecv, hsum, hrecv,
    q_ss, q_rs, do_ss, do_rs, kz_ss, kz_rs, ks_ss, ks_rs, loc,
    ea_ss, ea_rs, eu_ss, eu_rs, ed_ss, ed_rs, ec_ss, ec_rs,
    sx_ss, sx_rs, dq_ss, dq_rs, si_ss, si_rs, zz_ss, zz_rs, y_ss, y_rs, hh_ss, hh_rs, ld,
    etot, ertot, ztot, ztr_up, ztr_dn, et_ss, et_rs, ut_ss, ut_rs, dt_ss, dt_rs,
):
    channels = xb.shape[1]
    n_chunks = channels // CW
    slice_w = channels // PLANE
    c = lax.axis_index("ctx")
    g = lax.axis_index("grp")
    z = c // PLANE
    p = c % PLANE
    xx = p // 2
    core = p % 2
    sib = c + 1 - 2 * core
    base = z * PLANE
    y = g % 4
    gz = g - y

    def plane_peer(k):
        return (p + k) % PLANE

    def plane_from(k):
        return (p + PLANE - k) % PLANE

    def rcopy(src, dst, ss, rs, dev):
        return pltpu.make_async_remote_copy(
            src_ref=src, dst_ref=dst, send_sem=ss, recv_sem=rs, device_id=dev, device_id_type=MESH
        )

    bar = pltpu.get_barrier_semaphore()

    def greet(dev):
        pl.semaphore_signal(bar, inc=1, device_id=dev, device_id_type=MESH)

    greet({"grp": (g + 4) % 8})
    for k in (4, 3, 5, 2, 6, 1, 7):
        greet({"ctx": ((z + k) % NZ) * PLANE + p})
    for k in range(1, 4):
        greet({"grp": gz + (y + k) % 4})
    for k in range(1, PLANE):
        greet({"ctx": base + plane_peer(k)})

    key_rows = pl.ds(pl.multiple_of(core * TOK, TOK), TOK)
    loads = [
        pltpu.make_async_copy(src, dst, ld.at[i])
        for i, (src, dst) in enumerate((
            (st_ref, stb), (x_ref, xb), (gy_ref, gyb), (rate_ref, rates),
            (b_ref, bct.at[0:NST, :]), (c_ref, bct.at[NST:2 * NST, :]),
            (k_ref, kvg.at[z, key_rows, 0:HD]), (v_ref, kvg.at[z, key_rows, HD:2 * HD]),
        ))
    ]
    for load in loads:
        load.start()

    loads[4].wait()
    loads[5].wait()
    exact = bct[...]
    tmp[...] = jnp.zeros_like(tmp)
    for i in range(3):
        piece = exact.astype(BF16).astype(F32)
        tmp[2 * NST * i:2 * NST * (i + 1), :] = piece
        exact = exact - piece
    spr[...] = tmp[...].T
    own_state = (
        lax.broadcasted_iota(jnp.int32, (NST, 128), 1) % NST
        == lax.broadcasted_iota(jnp.int32, (NST, 128), 0)
    )
    pick = jnp.where(
        (lax.broadcasted_iota(jnp.int32, (128, 256), 0) // NST) % 2
        == lax.broadcasted_iota(jnp.int32, (128, 256), 1) // 128,
        1.0, 0.0,
    ).astype(BF16)

    def spread(i, _):
        rows = [
            jnp.where(own_state, jnp.broadcast_to(spr[pl.ds(8 * i + j, 1), :], (NST, 128)), 0.0)
            for j in range(8)
        ]
        both = dot(jnp.concatenate(rows, axis=0).astype(BF16), pick, ((1,), (0,)))
        at = pl.ds(pl.multiple_of(8 * i * NST, 8 * NST), 8 * NST)
        bb[at, :] = both[:, 0:128]
        cb[at, :] = both[:, 128:256]
        return 0

    lax.fori_loop(0, TOK // 8, spread, 0, unroll=4)
    for load in loads[0:4]:
        load.wait()
    stf[...] = stb[...].astype(F32)
    uf[...] = stf[...] * xb[...].astype(F32)
    gyf[...] = gyb[...].astype(F32)
    ratel[...] = rates[...] * (-LOG2E)
    def put_total(ref, row):
        for i in range(slice_w // 128):
            ref[i:i + 1, :] = row[:, i * 128:(i + 1) * 128]

    def get_total(ref):
        return jnp.concatenate([ref[i:i + 1, :] for i in range(slice_w // 128)], axis=1)

    earlier = jnp.where(
        lax.broadcasted_iota(jnp.int32, (TOK + 8, TOK), 0)
        > lax.broadcasted_iota(jnp.int32, (TOK + 8, TOK), 1),
        1.0, 0.0,
    ).astype(BF16)

    def first_chunk(ch, _):
        lanes = pl.ds(pl.multiple_of(ch * CW, CW), CW)
        rt = ratel[:, lanes]

        def body(i, carry):
            h, pr, gg = carry
            for j in range(8):
                t = 8 * i + j
                at = pl.ds(pl.multiple_of(t * NST, NST), NST)
                bt = jnp.tile(bb[at, :], (1, CW // 128))
                ct = jnp.tile(cb[at, :], (1, CW // 128))
                a = jnp.exp2(rt * stf[pl.ds(t, 1), lanes])
                avs[at, lanes] = a
                h = a * h + uf[pl.ds(t, 1), lanes] * bt
                hs[pl.ds(pl.multiple_of((t + 1) * NST, NST), NST), lanes] = h
                pr = a * pr
                gg = gg + pr * (gyf[pl.ds(t, 1), lanes] * ct)
            return (h, pr, gg)

        zero = jnp.zeros((NST, CW), F32)
        hs[0:NST, lanes] = zero
        h, pr, gg = lax.fori_loop(0, TOK // 8, body, (zero, jnp.ones((NST, CW), F32), zero))
        before = dot(earlier, stb[:, lanes], ((1,), (0,)))
        total = before[TOK:TOK + 1, :]
        cum[:, lanes] = before
        for half in range(CW // slice_w):
            to = ch * (CW // slice_w) + half
            cut = slice(half * slice_w, (half + 1) * slice_w)
            ebuf[to, 0:NST, :] = h[:, cut].astype(BF16)
            ebuf[to, NST:2 * NST, :] = gg[:, cut].astype(BF16)
            put_total(etot.at[to], total[:, cut])
        return 0

    lax.fori_loop(0, 1, first_chunk, 0)
    loads[6].wait()
    loads[7].wait()

    pl.semaphore_wait(bar, PLANE - 1 + NZ - 1 + 3 + 1)

    def q_copy(k, whole, gathered, ss, rs):
        dst = plane_peer(k)
        cols = pl.ds(pl.multiple_of((dst % 2) * 2 * HD, 2 * HD), 2 * HD)
        rows = pl.ds(pl.multiple_of(p * TOK, TOK), TOK)
        return rcopy(
            whole.at[:, cols], gathered.at[rows, :], ss.at[k], rs.at[k], {"ctx": base + dst}
        )

    def kv_part(slot, piece):
        at = core * TOK + piece * KV_ROWS
        return kvg.at[slot, pl.ds(pl.multiple_of(at, KV_ROWS), KV_ROWS), :]

    def kv_up(s, slot, piece):
        part = kv_part(slot, piece)
        return rcopy(part, part, kz_ss.at[s, piece], kz_rs.at[s + 1, piece], {"ctx": c + PLANE})

    def kv_over(s, slot):
        part = kvg.at[slot, pl.ds(pl.multiple_of(core * TOK, TOK), TOK), :]
        return rcopy(part, part, ks_ss.at[s], ks_rs.at[s], {"ctx": sib})

    def kv_step(s):
        slot = z - s

        @pl.when(slot >= 0)
        def _():
            for piece in range(TOK // KV_ROWS):
                @pl.when(s > 0)
                def _():
                    part = kv_part(slot, piece)
                    rcopy(
                        part, part, kz_ss.at[s, piece], kz_rs.at[s, piece], {"ctx": sib}
                    ).wait_recv()

                @pl.when(z < NZ - 1)
                def _():
                    kv_up(s, slot, piece).start()

            kv_over(s, slot).start()

    def kv_sib_wait(s):
        part = kvg.at[z - s, pl.ds(pl.multiple_of((1 - core) * TOK, TOK), TOK), :]
        rcopy(part, part, ks_ss.at[s], ks_rs.at[s], {"ctx": sib}).wait_recv()

    kv_step(jnp.int32(0))
    for k in range(1, PLANE):
        q_copy(k, q_ref, qg, q_ss, q_rs).start()
    my_cols = pl.ds(pl.multiple_of(core * 2 * HD, 2 * HD), 2 * HD)
    my_rows = pl.ds(pl.multiple_of(p * TOK, TOK), TOK)
    loc_q = pltpu.make_async_copy(q_ref.at[:, my_cols], qg.at[my_rows, :], loc.at[0])
    loc_do = pltpu.make_async_copy(do_ref.at[:, my_cols], dog.at[my_rows, :], loc.at[1])
    loc_q.start()
    loc_do.start()

    def first_step(ch, _):
        first_chunk(ch, 0)

        @pl.when(ch >= 2)
        def _():
            kv_step(ch - 1)

        return 0

    lax.fori_loop(1, n_chunks, first_step, 0)

    def e_copy(k):
        dst = plane_peer(k)
        return rcopy(ebuf.at[dst], erecv.at[p], ea_ss.at[k], ea_rs.at[k], {"ctx": base + dst})

    def et_copy(k):
        dst = plane_peer(k)
        return rcopy(etot.at[dst], ertot.at[p], et_ss.at[k], et_rs.at[k], {"ctx": base + dst})

    for k in range(1, PLANE):
        e_copy(k).start()
        et_copy(k).start()
    for k in range(1, PLANE):
        q_copy(k, do_ref, dog, do_ss, do_rs).start()
    erecv[p] = ebuf[p]
    ertot[p] = etot[p]

    mst[...] = jnp.full(mst.shape, NEG, F32)
    lst[...] = jnp.zeros_like(lst)
    rst[...] = jnp.zeros_like(rst)

    def tile_of(ch):
        head = ch // (1024 // ROWS)
        rows = pl.ds(pl.multiple_of((ch % (1024 // ROWS)) * ROWS, ROWS), ROWS)
        cols = pl.ds(pl.multiple_of(head * HD, HD), HD)
        lanes = pl.ds(pl.multiple_of(ch * ROWS, ROWS), ROWS)
        return rows, cols, lanes

    def seen(ch):
        key = xx * 2 * TOK + lax.broadcasted_iota(jnp.int32, (2 * TOK, ROWS), 0)
        query = (ch % (1024 // ROWS)) * ROWS + lax.broadcasted_iota(jnp.int32, (2 * TOK, ROWS), 1)
        return key <= query

    def attn_first(slot, diagonal):
        def body(ch, _):
            rows, cols, lanes = tile_of(ch)
            sc = dot(kvg[slot, :, 0:HD], qg[rows, cols], ((1,), (1,))) * (SCALE * LOG2E)
            if diagonal:
                sc = jnp.where(seen(ch), sc, NEG)
            sc = sc.reshape(2 * TOK // 8, 8, ROWS)
            dp = dot(kvg[slot, :, HD:2 * HD], dog[rows, cols], ((1,), (1,)))
            dp = dp.reshape(2 * TOK // 8, 8, ROWS)
            m_old = mst[:, lanes]
            m_new = jnp.maximum(m_old, jnp.max(sc, axis=0))
            shrink = jnp.exp2(m_old - m_new)
            pr = jnp.exp2(sc - m_new[None])
            mst[:, lanes] = m_new
            lst[:, lanes] = lst[:, lanes] * shrink + jnp.sum(pr, axis=0)
            rst[:, lanes] = rst[:, lanes] * shrink + jnp.sum(pr * dp, axis=0)
            return 0

        lax.fori_loop(0, 2 * 1024 // ROWS, body, 0, unroll=True)

    kv_step(jnp.int32(3))

    for k in range(1, PLANE):
        e_copy(k).wait()
        et_copy(k).wait()
    mine = pl.ds(pl.multiple_of(p * slice_w, slice_w), slice_w)
    rslice = ratel[:, mine]
    zero_s = jnp.zeros((NST, slice_w), F32)
    state = zero_s
    total = jnp.zeros((1, slice_w), F32)
    for j in range(PLANE):
        pre_f[j, 0:NST, :] = state
        pre_f[j, NST:2 * NST, :] = jnp.exp2(rslice * total)
        tj = get_total(ertot.at[j])
        state = jnp.exp2(rslice * tj) * state + erecv[j, 0:NST, :].astype(F32)
        total = total + tj
    plane_total = total
    zmsg_up[...] = state.astype(BF16)
    put_total(ztot, plane_total)
    state = zero_s
    total = jnp.zeros((1, slice_w), F32)
    for j in range(PLANE - 1, -1, -1):
        pre_b[j, 0:NST, :] = state
        pre_b[j, NST:2 * NST, :] = jnp.exp2(rslice * total)
        tj = get_total(ertot.at[j])
        state = jnp.exp2(rslice * tj) * state + erecv[j, NST:2 * NST, :].astype(F32)
        total = total + tj
    zmsg_dn[...] = state.astype(BF16)

    def up_copy(k):
        return rcopy(
            zmsg_up, zrecv_up.at[k], eu_ss.at[k], eu_rs.at[k], {"ctx": c + k * PLANE}
        )

    def dn_copy(k):
        return rcopy(
            zmsg_dn, zrecv_dn.at[k], ed_ss.at[k], ed_rs.at[k], {"ctx": c - k * PLANE}
        )

    def upt_copy(k):
        return rcopy(ztot, ztr_up.at[k], ut_ss.at[k], ut_rs.at[k], {"ctx": c + k * PLANE})

    def dnt_copy(k):
        return rcopy(ztot, ztr_dn.at[k], dt_ss.at[k], dt_rs.at[k], {"ctx": c - k * PLANE})

    for k in range(1, NZ):
        @pl.when(z + k < NZ)
        def _(k=k):
            upt_copy(k).start()
            up_copy(k).start()

        @pl.when(z - k >= 0)
        def _(k=k):
            dnt_copy(k).start()
            dn_copy(k).start()

    kv_step(jnp.int32(4))
    for k in range(1, PLANE):
        q_copy(k, q_ref, qg, q_ss, q_rs).wait()
        q_copy(k, do_ref, dog, do_ss, do_rs).wait()
    loc_q.wait()
    loc_do.wait()
    kv_sib_wait(jnp.int32(0))
    attn_first(z, True)
    kv_step(jnp.int32(5))

    def attn_step(s, _):
        kv_sib_wait(s)
        attn_first(z - s, False)

        @pl.when(s <= 2)
        def _():
            kv_step(s + 5)

        return 0

    near = jnp.minimum(z, 3)
    lax.fori_loop(1, near + 1, attn_step, 0)

    sin_f[...] = zero_s
    sin_b[...] = zero_s
    for k in range(NZ - 1, 0, -1):
        @pl.when(z - k >= 0)
        def _(k=k):
            rcopy(
                zmsg_up, zrecv_up.at[k], eu_ss.at[k], eu_rs.at[k], {"ctx": sib}
            ).wait_recv()
            rcopy(ztot, ztr_up.at[k], ut_ss.at[k], ut_rs.at[k], {"ctx": sib}).wait_recv()
            dec = jnp.exp2(rslice * get_total(ztr_up.at[k]))
            sin_f[...] = dec * sin_f[...] + zrecv_up[k].astype(F32)

        @pl.when(z + k < NZ)
        def _(k=k):
            rcopy(
                zmsg_dn, zrecv_dn.at[k], ed_ss.at[k], ed_rs.at[k], {"ctx": sib}
            ).wait_recv()
            rcopy(ztot, ztr_dn.at[k], dt_ss.at[k], dt_rs.at[k], {"ctx": sib}).wait_recv()
            dec = jnp.exp2(rslice * get_total(ztr_dn.at[k]))
            sin_b[...] = dec * sin_b[...] + zrecv_dn[k].astype(F32)
    for j in range(PLANE):
        cbuf[j, 0:NST, :] = (
            pre_f[j, 0:NST, :] + pre_f[j, NST:2 * NST, :] * sin_f[...]
        ).astype(BF16)
        cbuf[j, NST:2 * NST, :] = (
            pre_b[j, 0:NST, :] + pre_b[j, NST:2 * NST, :] * sin_b[...]
        ).astype(BF16)

    def c_copy(k):
        dst = plane_peer(k)
        return rcopy(cbuf.at[dst], crecv.at[p], ec_ss.at[k], ec_rs.at[k], {"ctx": base + dst})

    for k in range(1, PLANE):
        c_copy(k).start()
    crecv[p] = cbuf[p]

    lax.fori_loop(near + 1, z + 1, attn_step, 0)

    m8 = mst[...]
    m1 = jnp.max(m8, axis=0, keepdims=True)
    w8 = jnp.exp2(m8 - m1)
    l1 = jnp.sum(lst[...] * w8, axis=0, keepdims=True)
    r1 = jnp.sum(rst[...] * w8, axis=0, keepdims=True)
    n_rt = 2 * 1024 // 128
    for j in range(n_rt):
        cut = slice(j * 128, (j + 1) * 128)
        stat[0, j:j + 1, :] = m1[:, cut]
        stat[0, n_rt + j:n_rt + j + 1, :] = l1[:, cut]
        stat[0, 2 * n_rt + j:2 * n_rt + j + 1, :] = r1[:, cut]

    def stat_copy(k):
        dst = base + ((xx + k) % 4) * 2 + core
        return rcopy(stat.at[0], stat.at[k], sx_ss.at[k], sx_rs.at[k], {"ctx": dst})

    for k in range(1, 4):
        stat_copy(k).start()

    def second_chunk(ch, _):
        lanes = pl.ds(pl.multiple_of(ch * CW, CW), CW)
        rt = ratel[:, lanes]
        per = CW // slice_w
        h_in = jnp.concatenate([crecv[ch * per + i, 0:NST, :] for i in range(per)], axis=1).astype(F32)
        g_in = jnp.concatenate([crecv[ch * per + i, NST:2 * NST, :] for i in range(per)], axis=1).astype(F32)
        h_end = hs[TOK * NST:(TOK + 1) * NST, lanes] + jnp.exp2(
            rt * cum[TOK:TOK + 1, lanes]
        ) * h_in

        def folded(v):
            out = v[:, 0:128]
            for i in range(1, CW // 128):
                out = out + v[:, i * 128:(i + 1) * 128]
            return out

        def backward(i, both):
            carry, h_now = both
            lo = TOK // 8 - 1 - i
            for j in range(7, -1, -1):
                t = 8 * lo + j
                at = pl.ds(pl.multiple_of(t * NST, NST), NST)
                bt = jnp.tile(bb[at, :], (1, CW // 128))
                ct = jnp.tile(cb[at, :], (1, CW // 128))
                gyt = gyf[pl.ds(t, 1), lanes]
                gn = ct * gyt + carry
                carry = avs[at, lanes] * gn
                h_before = hs[at, lanes] + jnp.exp2(rt * cum[pl.ds(t, 1), lanes]) * h_in
                qv = carry * rt * h_before
                gb = gn * bt
                for v in range(CW // 128):
                    cut = slice(v * 128, (v + 1) * 128)
                    sg[v, j * 8:(j + 1) * 8, :] = gb[0:8, cut] + gb[8:16, cut]
                    sq[v, j * 8:(j + 1) * 8, :] = qv[0:8, cut] + qv[8:16, cut]
                wacc[at, :] += folded(gn * uf[pl.ds(t, 1), lanes])
                racc[at, :] += folded(h_now * gyt)
                h_now = h_before
            rows = pl.ds(pl.multiple_of(8 * lo, 8), 8)
            for v in range(CW // 128):
                cut = slice(v * 128, (v + 1) * 128)
                a1 = sg[v, pl.ds(0, 8, stride=8), :]
                a2 = sq[v, pl.ds(0, 8, stride=8), :]
                for n in range(1, 8):
                    a1 = a1 + sg[v, pl.ds(n, 8, stride=8), :]
                    a2 = a2 + sq[v, pl.ds(n, 8, stride=8), :]
                s1[rows, cut] = a1
                s2[rows, cut] = a2
            return carry, h_now

        lax.fori_loop(0, TOK // 8, backward, (g_in, h_end))
        gx_ref[:, lanes] = (s1[...] * stf[:, lanes]).astype(BF16)
        gs_ref[:, lanes] = (
            s1[...] * xb[:, lanes].astype(F32) + LN2 * s2[...]
        ).astype(BF16)
        return 0

    def y_copy(k):
        return rcopy(wred, yrecv.at[k], y_ss.at[k], y_rs.at[k], {"grp": gz + (y + k) % 4})

    h_copy = rcopy(hsum, hrecv, hh_ss, hh_rs, {"grp": (g + 4) % 8})

    def states_here():
        for k in range(1, PLANE):
            c_copy(k).wait()
        wacc[...] = jnp.zeros_like(wacc)
        racc[...] = jnp.zeros_like(racc)

    def coefficients():
        ones = jnp.ones((8, 256), BF16)
        for n in range(NST):
            for acc, to in ((wacc, n), (racc, NST + n)):
                part = acc[pl.ds(n, TOK, stride=NST), :]
                high = part.astype(BF16)
                low = (part - high.astype(F32)).astype(BF16)
                total = dot(ones, jnp.concatenate([high, low], axis=1), ((1,), (1,)))
                wred[to:to + 1, :] = total[0:1, :]

        for k in range(1, 4):
            y_copy(k).start()

    def across_z_hi():
        for k in range(1, 4):
            y_copy(k).wait()
        hsum[...] = wred[...] + yrecv[1] + yrecv[2] + yrecv[3]
        h_copy.start()

    def all_stats():
        for k in range(1, 4):
            stat_copy(k).wait()
        m4 = [stat[k, 0:n_rt, :] for k in range(4)]
        m_all = jnp.maximum(jnp.maximum(m4[0], m4[1]), jnp.maximum(m4[2], m4[3]))
        l_all = jnp.zeros((n_rt, 128), F32)
        r_all = jnp.zeros((n_rt, 128), F32)
        for k in range(4):
            w = jnp.exp2(m4[k] - m_all)
            l_all = l_all + w * stat[k, n_rt:2 * n_rt, :]
            r_all = r_all + w * stat[k, 2 * n_rt:3 * n_rt, :]
        lse_t = m_all + jnp.log2(l_all)
        rd_t = r_all / l_all
        for j in range(n_rt):
            cut = slice(j * 128, (j + 1) * 128)
            lse[:, cut] = jnp.broadcast_to(lse_t[j:j + 1, :], (8, 128))
            rdt[:, cut] = jnp.broadcast_to(rd_t[j:j + 1, :], (8, 128))

    dqt[...] = jnp.zeros_like(dqt)

    def attn_second(s, slot, diagonal):
        keys_t = kvg[slot, :, 0:HD].T

        def body(ch, carry):
            dk, dv = carry
            rows, cols, lanes = tile_of(ch)
            keys = kvg[slot, :, 0:HD]
            sc = dot(keys, qg[rows, cols], ((1,), (1,))) * (SCALE * LOG2E)
            pr = jnp.exp2(sc.reshape(2 * TOK // 8, 8, ROWS) - lse[:, lanes][None])
            if diagonal:
                pr = jnp.where(seen(ch).reshape(pr.shape), pr, 0.0)
            dp = dot(kvg[slot, :, HD:2 * HD], dog[rows, cols], ((1,), (1,)))
            ds = pr * (dp.reshape(pr.shape) - rdt[:, lanes][None])
            pb = pr.reshape(2 * TOK, ROWS).astype(BF16)
            db = ds.reshape(2 * TOK, ROWS).astype(BF16)
            dv = dv + dot(pb, dog[rows, cols], ((1,), (0,)))
            dk = dk + dot(db, qg[rows, cols], ((1,), (0,)))
            head = pl.ds(pl.multiple_of((ch // (1024 // ROWS)) * HD, HD), HD)
            dqt[head, rows] += dot(keys_t, db, ((1,), (0,)))
            return dk, dv

        zero = jnp.zeros((2 * TOK, HD), F32)
        dk, dv = lax.fori_loop(0, 2 * 1024 // ROWS, body, (zero, zero), unroll=True)
        dk = dk * SCALE
        first = core == 0
        own[s, :, 0:HD] = jnp.where(first, dk[0:TOK], dk[TOK:])
        own[s, :, HD:2 * HD] = jnp.where(first, dv[0:TOK], dv[TOK:])
        sib_s[s, :, 0:HD] = jnp.where(first, dk[TOK:], dk[0:TOK])
        sib_s[s, :, HD:2 * HD] = jnp.where(first, dv[TOK:], dv[0:TOK])
        sib_copy(s).start()

    def sib_copy(s):
        return rcopy(sib_s.at[s], sib_r.at[s], si_ss.at[s], si_rs.at[s], {"ctx": sib})

    def z_copy(s):
        return rcopy(
            zs.at[s], zr.at[s], zz_ss.at[s], zz_rs.at[s], {"ctx": c - s * PLANE}
        )

    def hand_down(s):
        sib_copy(s).wait()
        zs[s] = (own[s] + sib_r[s]).astype(BF16)
        z_copy(s).start()

    turn = jnp.maximum(z - 3, 0)

    def second_step(i, _):
        s = z - i

        @pl.when(i == 0)
        def _():
            states_here()

        @pl.when(jnp.logical_or(i == 0, i == turn))
        def _():
            first = jnp.where(i == 0, 0, 1)
            last = jnp.where(i == turn, n_chunks, 1)
            lax.fori_loop(first, last, second_chunk, 0)

        @pl.when(i == turn)
        def _():
            coefficients()

        @pl.when(i == 0)
        def _():
            all_stats()

        @pl.when(i < z)
        def _():
            attn_second(s, z - s, False)

        @pl.when(i == z)
        def _():
            attn_second(jnp.int32(0), z, True)

        @pl.when(i > 0)
        def _():
            hand_down(s + 1)

        @pl.when(i == jnp.minimum(turn + 2, z))
        def _():
            across_z_hi()

        return 0

    lax.fori_loop(0, z + 1, second_step, 0)

    dqs[...] = (dqt[...] * SCALE).astype(BF16)

    def dq_copy(k):
        dst = plane_peer(k)
        cols = pl.ds(pl.multiple_of(dst * TOK, TOK), TOK)
        return rcopy(
            dqs.at[:, cols], dqr.at[p], dq_ss.at[k], dq_rs.at[k], {"ctx": base + dst}
        )

    for k in range(1, PLANE):
        dq_copy(k).start()
    own_dq = pltpu.make_async_copy(
        dqs.at[:, pl.ds(pl.multiple_of(p * TOK, TOK), TOK)], dqr.at[p], loc.at[4]
    )
    own_dq.start()
    sib_copy(jnp.int32(0)).wait()

    for k in range(1, PLANE):
        dq_copy(k).wait()
    own_dq.wait()
    for cc in range(2):
        tot = dqr[cc].astype(F32)
        for i in range(1, 4):
            tot = tot + dqr[2 * i + cc].astype(F32)
        for h in range(2):
            col = (cc * 2 + h) * HD
            dq_ref[:, col:col + HD] = tot[h * HD:(h + 1) * HD, :].T.astype(BF16)

    own[0] = own[0] + sib_r[0]
    for k in range(1, NZ):
        @pl.when(z + k < NZ)
        def _(k=k):
            rcopy(zs.at[k], zr.at[k], zz_ss.at[k], zz_rs.at[k], {"ctx": sib}).wait_recv()
            own[0] = own[0] + zr[k].astype(F32)
    dk_ref[...] = own[0, :, 0:HD].astype(BF16)
    dv_ref[...] = own[0, :, HD:2 * HD].astype(BF16)

    h_copy.wait()
    gw_ref[...] = hsum[0:NST, :] + hrecv[0:NST, :]
    gr_ref[...] = hsum[NST:2 * NST, :] + hrecv[NST:2 * NST, :]

    for k in range(1, NZ):
        @pl.when(z + k < NZ)
        def _(k=k):
            up_copy(k).wait_send()
            upt_copy(k).wait_send()

        @pl.when(z - k >= 0)
        def _(k=k):
            dn_copy(k).wait_send()
            dnt_copy(k).wait_send()
            z_copy(k).wait_send()
    for s in range(NZ):
        @pl.when(z - s >= 0)
        def _(s=s):
            kv_over(s, z - s).wait_send()

            @pl.when(z < NZ - 1)
            def _():
                for piece in range(TOK // KV_ROWS):
                    kv_up(s, z - s, piece).wait_send()


def hand_over(*refs):
    copies = [pltpu.make_async_copy(refs[i], refs[7 + i], refs[14].at[i]) for i in range(7)]
    for copy in copies:
        copy.start()
    for copy in copies:
        copy.wait()


def on_device(
    queries, key_vectors, value_vectors, grad_attn, mamba_input, step_sizes, decay_rates,
    write_coef, read_coef, grad_mamba,
):
    channels = mamba_input.shape[1]
    slice_w = channels // PLANE
    vmem = pltpu.VMEM
    dma = pltpu.SemaphoreType.DMA
    scratch = [
        vmem((TOK, channels), BF16), vmem((TOK, channels), BF16), vmem((TOK, channels), BF16),
        vmem((NST, channels), F32), vmem((2 * NST, TOK), F32), vmem((128, 128), F32),
        vmem((1024, 256), BF16), vmem((1024, 256), BF16), vmem((NZ, 256, 256), BF16),
        vmem((TOK, channels), F32), vmem((TOK, channels), F32), vmem((TOK, channels), F32),
        vmem((TOK * NST, 128), F32), vmem((TOK * NST, 128), F32), vmem((128, 128), F32),
        vmem((NST, channels), F32),
        vmem((PLANE, 32, slice_w), BF16), vmem((PLANE, 32, slice_w), BF16),
        vmem((NST, slice_w), BF16), vmem((NST, slice_w), BF16),
        vmem((NZ, NST, slice_w), BF16), vmem((NZ, NST, slice_w), BF16),
        vmem((PLANE, 32, slice_w), F32), vmem((PLANE, 32, slice_w), F32),
        vmem((NST, slice_w), F32), vmem((NST, slice_w), F32),
        vmem((PLANE, 32, slice_w), BF16), vmem((PLANE, 32, slice_w), BF16),
        vmem((8, 2048), F32), vmem((8, 2048), F32), vmem((8, 2048), F32),
        vmem((4, 48, 128), F32), vmem((8, 2048), F32), vmem((8, 2048), F32),
        vmem((256, 1024), F32), vmem((256, 1024), BF16), vmem((PLANE, 256, 128), BF16),
        vmem((NZ, 128, 256), F32), vmem((NZ, 128, 256), F32), vmem((NZ, 128, 256), F32),
        vmem((NZ, 128, 256), BF16), vmem((NZ, 128, 256), BF16),
        vmem(((TOK + 1) * NST, channels), F32), vmem((TOK * NST, channels), F32),
        vmem((TOK + 8, channels), F32),
        vmem((CW // 128, 64, 128), F32), vmem((CW // 128, 64, 128), F32), vmem((TOK, CW), F32), vmem((TOK, CW), F32),
        vmem((TOK * NST, 128), F32), vmem((TOK * NST, 128), F32),
        vmem((32, 128), F32), vmem((4, 32, 128), F32), vmem((32, 128), F32), vmem((32, 128), F32),
        dma((8,)), dma((8,)), dma((8,)), dma((8,)),
        dma((8, TOK // KV_ROWS)), dma((8, TOK // KV_ROWS)), dma((8,)), dma((8,)),
        dma((8,)),
        dma((8,)), dma((8,)), dma((8,)), dma((8,)), dma((8,)), dma((8,)), dma((8,)), dma((8,)),
        dma((4,)), dma((4,)), dma((8,)), dma((8,)), dma((8,)), dma((8,)), dma((8,)), dma((8,)),
        dma((4,)), dma((4,)), dma, dma, dma((8,)),
        vmem((PLANE, slice_w // 128, 128), F32), vmem((PLANE, slice_w // 128, 128), F32),
        vmem((slice_w // 128, 128), F32),
        vmem((NZ, slice_w // 128, 128), F32), vmem((NZ, slice_w // 128, 128), F32),
        dma((8,)), dma((8,)), dma((8,)), dma((8,)), dma((8,)), dma((8,)),
    ]
    outs = (
        jax.ShapeDtypeStruct(queries.shape, BF16),
        jax.ShapeDtypeStruct(key_vectors.shape, BF16),
        jax.ShapeDtypeStruct(value_vectors.shape, BF16),
        jax.ShapeDtypeStruct(mamba_input.shape, BF16),
        jax.ShapeDtypeStruct(step_sizes.shape, BF16),
        jax.ShapeDtypeStruct((NST, TOK), F32),
        jax.ShapeDtypeStruct((NST, TOK), F32),
    )
    made = pl.pallas_call(
        kernel,
        out_shape=outs,
        in_specs=[pl.BlockSpec(memory_space=pl.ANY)] * 10,
        out_specs=(pl.BlockSpec(memory_space=pltpu.VMEM),) * 7,
        scratch_shapes=scratch,
        compiler_params=pltpu.CompilerParams(
            collective_id=0, has_side_effects=True, vmem_limit_bytes=60 * 2**20
        ),
    )(
        queries, key_vectors, value_vectors, grad_attn, mamba_input, step_sizes, decay_rates,
        write_coef.T, read_coef.T, grad_mamba,
    )
    out = pl.pallas_call(
        hand_over,
        out_shape=outs,
        in_specs=[pl.BlockSpec(memory_space=pltpu.VMEM)] * 7,
        out_specs=(pl.BlockSpec(memory_space=pltpu.HBM),) * 7,
        scratch_shapes=[dma((7,))],
    )(*made)
    return out[:5] + (out[5].T, out[6].T)


def solution(mesh):
    both = P("ctx", "grp")
    rows = P("ctx", None)
    return jax.shard_map(
        on_device,
        mesh=mesh,
        in_specs=(both,) * 6 + (P(None, "grp"), rows, rows, both),
        out_specs=(both,) * 5 + (rows, rows),
        check_vma=False,
    )
```

time: 110 us -> 79.7 us (0.72)
  the two profiles are of different devices: /device:TPU:486 before, /device:TPU:105 now
where the time goes in v2:
time: 79.7 us; the launch traced here: 79.5 us
  Pallas kernels  78.9 us (99%)
    pallas_call x1, Pallas kernels, on_device(): pl.pallas_call(kernel, out_shape=outs, in_specs=[pl.BlockSpec(memory_spac...  76.5 us
    pallas_call x1, Pallas kernels, on_device(): pl.pallas_call(hand_over, out_shape=outs, in_specs=[pl.BlockSpec(memory_s...  2.39 us

profile of v2, /device:TPU:105, one launch (start us, length us, event | category | flops | bytes accessed | tf_op | source)
XLA Modules:
  0.0 79.5 jit_solution(15251226142621739631)
XLA Ops:
  0.6 76.5 %shard_map.153 = (bf16[128,512]{1,0:T(8,128)(2,1)}, bf16[128,128]{1,0:T(8,128)(2,1)}, bf16[128,128]{1,0:T(8,128)(2,1)}, bf16[128,2048]{1,0:T(8,128)(2,1)}, bf16[...) custom-call(bf16[128,512]{1,0:T(8,128)(2,1)} %q_ref.1, bf16[128,128]{1,0:T(8,128)(2,1)} %k_ref.1, ...), custom_call_target="tpu_custom_call" | custom-call | tf_op jit(solution)/shard_map/pallas_call | solution.py:750
  77.1 2.4 %shard_map.154 = (bf16[128,512]{1,0:T(8,128)(2,1)}, bf16[128,128]{1,0:T(8,128)(2,1)}, bf16[128,128]{1,0:T(8,128)(2,1)}, bf16[128,2048]{1,0:T(8,128)(2,1)}, bf16[...) custom-call(bf16[128,512]{1,0:T(8,128)(2,1)} %get-tuple-element.21.refs_0_, ...), custom_call_target="tpu_custom_call" | custom-call | tf_op jit(solution)/shard_map/pallas_call | solution.py:763

commit v3 on v2

--- a/solution.py
+++ b/solution.py
@@ -21,6 +21,7 @@
 NEG = -1e30
 CW = 512
 ROWS = 512
+FAR = 4
 KV_ROWS = 32
 
 
@@ -31,12 +32,12 @@
 def kernel(
     q_ref, k_ref, v_ref, do_ref, x_ref, st_ref, rate_ref, b_ref, c_ref, gy_ref,
     dq_ref, dk_ref, dv_ref, gx_ref, gs_ref, gw_ref, gr_ref,
-    xb, stb, gyb, rates, bct, spr, qg, dog, kvg, stf, uf, gyf, bb, cb, tmp, ratel,
+    gxb, gsb, xb, stb, gyb, rates, bct, spr, qg, dog, kvg, stf, uf, gyf, bb, cb, tmp, ratel,
     ebuf, erecv, zmsg_up, zmsg_dn, zrecv_up, zrecv_dn, pre_f, pre_b, sin_f, sin_b, cbuf, crecv,
     mst, lst, rst, stat, lse, rdt,
     dqt, dqs, dqr, own, sib_s, sib_r, zs, zr,
     hs, avs, cum, sg, sq, s1, s2, wacc, racc, wred, yrecv, hsum, hrecv,
-    q_ss, q_rs, do_ss, do_rs, kz_ss, kz_rs, ks_ss, ks_rs, loc,
+    q_ss, q_rs, do_ss, do_rs, kz_ss, kz_rs, kf_ss, ks_ss, ks_rs, loc,
     ea_ss, ea_rs, eu_ss, eu_rs, ed_ss, ed_rs, ec_ss, ec_rs,
     sx_ss, sx_rs, dq_ss, dq_rs, si_ss, si_rs, zz_ss, zz_rs, y_ss, y_rs, hh_ss, hh_rs, ld,
     etot, ertot, ztot, ztr_up, ztr_dn, et_ss, et_rs, ut_ss, ut_rs, dt_ss, dt_rs,
@@ -71,14 +72,6 @@
     def greet(dev):
         pl.semaphore_signal(bar, inc=1, device_id=dev, device_id_type=MESH)
 
-    greet({"grp": (g + 4) % 8})
-    for k in (4, 3, 5, 2, 6, 1, 7):
-        greet({"ctx": ((z + k) % NZ) * PLANE + p})
-    for k in range(1, 4):
-        greet({"grp": gz + (y + k) % 4})
-    for k in range(1, PLANE):
-        greet({"ctx": base + plane_peer(k)})
-
     key_rows = pl.ds(pl.multiple_of(core * TOK, TOK), TOK)
     loads = [
         pltpu.make_async_copy(src, dst, ld.at[i])
@@ -88,7 +81,16 @@
             (k_ref, kvg.at[z, key_rows, 0:HD]), (v_ref, kvg.at[z, key_rows, HD:2 * HD]),
         ))
     ]
-    for load in loads:
+    loads[4].start()
+    loads[5].start()
+    greet({"grp": (g + 4) % 8})
+    for k in (4, 3, 5, 2, 6, 1, 7):
+        greet({"ctx": ((z + k) % NZ) * PLANE + p})
+    for k in range(1, 4):
+        greet({"grp": gz + (y + k) % 4})
+    for k in range(1, PLANE):
+        greet({"ctx": base + plane_peer(k)})
+    for load in loads[0:4] + loads[6:8]:
         load.start()
 
     loads[4].wait()
@@ -196,6 +198,12 @@
         part = kv_part(slot, piece)
         return rcopy(part, part, kz_ss.at[s, piece], kz_rs.at[s + 1, piece], {"ctx": c + PLANE})
 
+    def kv_far(piece):
+        part = kv_part(z, piece)
+        return rcopy(
+            part, part, kf_ss.at[piece], kz_rs.at[FAR, piece], {"ctx": c + FAR * PLANE}
+        )
+
     def kv_over(s, slot):
         part = kvg.at[slot, pl.ds(pl.multiple_of(core * TOK, TOK), TOK), :]
         return rcopy(part, part, ks_ss.at[s], ks_rs.at[s], {"ctx": sib})
@@ -213,7 +221,7 @@
                         part, part, kz_ss.at[s, piece], kz_rs.at[s, piece], {"ctx": sib}
                     ).wait_recv()
 
-                @pl.when(z < NZ - 1)
+                @pl.when(jnp.logical_and(z < NZ - 1, s != FAR - 1))
                 def _():
                     kv_up(s, slot, piece).start()
 
@@ -224,6 +232,7 @@
         rcopy(part, part, ks_ss.at[s], ks_rs.at[s], {"ctx": sib}).wait_recv()
 
     kv_step(jnp.int32(0))
+
     for k in range(1, PLANE):
         q_copy(k, q_ref, qg, q_ss, q_rs).start()
     my_cols = pl.ds(pl.multiple_of(core * 2 * HD, 2 * HD), 2 * HD)
@@ -236,9 +245,14 @@
     def first_step(ch, _):
         first_chunk(ch, 0)
 
-        @pl.when(ch >= 2)
-        def _():
-            kv_step(ch - 1)
+        @pl.when(jnp.logical_and(ch == 1, z < NZ - FAR))
+        def _():
+            for piece in range(TOK // KV_ROWS):
+                kv_far(piece).start()
+
+        @pl.when(ch == 2)
+        def _():
+            kv_step(jnp.int32(1))
 
         return 0
 
@@ -296,11 +310,14 @@
 
         lax.fori_loop(0, 2 * 1024 // ROWS, body, 0, unroll=True)
 
+    kv_step(jnp.int32(2))
+    kv_step(jnp.int32(4))
     kv_step(jnp.int32(3))
 
     for k in range(1, PLANE):
         e_copy(k).wait()
         et_copy(k).wait()
+    kv_step(jnp.int32(5))
     mine = pl.ds(pl.multiple_of(p * slice_w, slice_w), slice_w)
     rslice = ratel[:, mine]
     zero_s = jnp.zeros((NST, slice_w), F32)
@@ -352,7 +369,6 @@
             dnt_copy(k).start()
             dn_copy(k).start()
 
-    kv_step(jnp.int32(4))
     for k in range(1, PLANE):
         q_copy(k, q_ref, qg, q_ss, q_rs).wait()
         q_copy(k, do_ref, dog, do_ss, do_rs).wait()
@@ -360,15 +376,15 @@
     loc_do.wait()
     kv_sib_wait(jnp.int32(0))
     attn_first(z, True)
-    kv_step(jnp.int32(5))
+    kv_step(jnp.int32(6))
 
     def attn_step(s, _):
         kv_sib_wait(s)
         attn_first(z - s, False)
 
-        @pl.when(s <= 2)
-        def _():
-            kv_step(s + 5)
+        @pl.when(s == 5)
+        def _():
+            kv_step(jnp.int32(7))
 
         return 0
 
@@ -482,8 +498,8 @@
             return carry, h_now
 
         lax.fori_loop(0, TOK // 8, backward, (g_in, h_end))
-        gx_ref[:, lanes] = (s1[...] * stf[:, lanes]).astype(BF16)
-        gs_ref[:, lanes] = (
+        gxb[:, lanes] = (s1[...] * stf[:, lanes]).astype(BF16)
+        gsb[:, lanes] = (
             s1[...] * xb[:, lanes].astype(F32) + LN2 * s2[...]
         ).astype(BF16)
         return 0
@@ -499,7 +515,12 @@
         wacc[...] = jnp.zeros_like(wacc)
         racc[...] = jnp.zeros_like(racc)
 
+    gx_out = pltpu.make_async_copy(gxb, gx_ref, loc.at[5])
+    gs_out = pltpu.make_async_copy(gsb, gs_ref, loc.at[6])
+
     def coefficients():
+        gx_out.start()
+        gs_out.start()
         ones = jnp.ones((8, 256), BF16)
         for n in range(NST):
             for acc, to in ((wacc, n), (racc, NST + n)):
@@ -582,7 +603,7 @@
         zs[s] = (own[s] + sib_r[s]).astype(BF16)
         z_copy(s).start()
 
-    turn = jnp.maximum(z - 3, 0)
+    turn = jnp.maximum(z - 2, 0)
 
     def second_step(i, _):
         s = z - i
@@ -662,6 +683,8 @@
     dk_ref[...] = own[0, :, 0:HD].astype(BF16)
     dv_ref[...] = own[0, :, HD:2 * HD].astype(BF16)
 
+    gx_out.wait()
+    gs_out.wait()
     h_copy.wait()
     gw_ref[...] = hsum[0:NST, :] + hrecv[0:NST, :]
     gr_ref[...] = hsum[NST:2 * NST, :] + hrecv[NST:2 * NST, :]
@@ -682,10 +705,16 @@
         def _(s=s):
             kv_over(s, z - s).wait_send()
 
-            @pl.when(z < NZ - 1)
-            def _():
-                for piece in range(TOK // KV_ROWS):
-                    kv_up(s, z - s, piece).wait_send()
+            if s != FAR - 1:
+                @pl.when(z < NZ - 1)
+                def _():
+                    for piece in range(TOK // KV_ROWS):
+                        kv_up(s, z - s, piece).wait_send()
+
+    @pl.when(z < NZ - FAR)
+    def _():
+        for piece in range(TOK // KV_ROWS):
+            kv_far(piece).wait_send()
 
 
 def hand_over(*refs):
@@ -705,6 +734,7 @@
     vmem = pltpu.VMEM
     dma = pltpu.SemaphoreType.DMA
     scratch = [
+        vmem((TOK, channels), BF16), vmem((TOK, channels), BF16),
         vmem((TOK, channels), BF16), vmem((TOK, channels), BF16), vmem((TOK, channels), BF16),
         vmem((NST, channels), F32), vmem((2 * NST, TOK), F32), vmem((128, 128), F32),
         vmem((1024, 256), BF16), vmem((1024, 256), BF16), vmem((NZ, 256, 256), BF16),
@@ -728,7 +758,8 @@
         vmem((TOK * NST, 128), F32), vmem((TOK * NST, 128), F32),
         vmem((32, 128), F32), vmem((4, 32, 128), F32), vmem((32, 128), F32), vmem((32, 128), F32),
         dma((8,)), dma((8,)), dma((8,)), dma((8,)),
-        dma((8, TOK // KV_ROWS)), dma((8, TOK // KV_ROWS)), dma((8,)), dma((8,)),
+        dma((8, TOK // KV_ROWS)), dma((8, TOK // KV_ROWS)), dma((TOK // KV_ROWS,)),
+        dma((8,)), dma((8,)),
         dma((8,)),
         dma((8,)), dma((8,)), dma((8,)), dma((8,)), dma((8,)), dma((8,)), dma((8,)), dma((8,)),
         dma((4,)), dma((4,)), dma((8,)), dma((8,)), dma((8,)), dma((8,)), dma((8,)), dma((8,)),
@@ -751,7 +782,9 @@
         kernel,
         out_shape=outs,
         in_specs=[pl.BlockSpec(memory_space=pl.ANY)] * 10,
-        out_specs=(pl.BlockSpec(memory_space=pltpu.VMEM),) * 7,
+        out_specs=(pl.BlockSpec(memory_space=pltpu.VMEM),) * 3
+        + (pl.BlockSpec(memory_space=pl.ANY),) * 2
+        + (pl.BlockSpec(memory_space=pltpu.VMEM),) * 2,
         scratch_shapes=scratch,
         compiler_params=pltpu.CompilerParams(
             collective_id=0, has_side_effects=True, vmem_limit_bytes=60 * 2**20

time: 79.7 us -> 80.8 us (1.014)
  the two profiles are of different devices: /device:TPU:105 before, /device:TPU:97 now
where the time goes in v3:
time: 80.8 us; the launch traced here: 80.6 us
  Pallas kernels  80 us (99%)
    pallas_call x1, Pallas kernels, on_device(): pl.pallas_call(kernel, out_shape=outs, in_specs=[pl.BlockSpec(memory_spac...  77.6 us
    pallas_call x1, Pallas kernels, on_device(): pl.pallas_call(hand_over, out_shape=outs, in_specs=[pl.BlockSpec(memory_s...  2.39 us

profile of v3, /device:TPU:97, one launch (start us, length us, event | category | flops | bytes accessed | tf_op | source)
XLA Modules:
  0.0 80.6 jit_solution(13229547542215870456)
XLA Ops:
  0.6 77.6 %shard_map.153 = (bf16[128,512]{1,0:T(8,128)(2,1)}, bf16[128,128]{1,0:T(8,128)(2,1)}, bf16[128,128]{1,0:T(8,128)(2,1)}, bf16[128,2048]{1,0:T(8,128)(2,1)}, bf16[...) custom-call(bf16[128,512]{1,0:T(8,128)(2,1)} %q_ref.1, bf16[128,128]{1,0:T(8,128)(2,1)} %k_ref.1, ...), custom_call_target="tpu_custom_call" | custom-call | tf_op jit(solution)/shard_map/pallas_call | solution.py:781
  78.3 2.4 %shard_map.154 = (bf16[128,512]{1,0:T(8,128)(2,1)}, bf16[128,128]{1,0:T(8,128)(2,1)}, bf16[128,128]{1,0:T(8,128)(2,1)}, bf16[128,2048]{1,0:T(8,128)(2,1)}, bf16[...) custom-call(bf16[128,512]{1,0:T(8,128)(2,1)} %get-tuple-element.21.refs_0_, ...), custom_call_target="tpu_custom_call" | custom-call | tf_op jit(solution)/shard_map/pallas_call | solution.py:796

commit v4 on v3

--- a/solution.py
+++ b/solution.py
@@ -21,6 +21,7 @@
 NEG = -1e30
 CW = 512
 ROWS = 512
+FIRST_FAR = (4, 3, 5, 2, 6, 1, 7)
 FAR = 4
 KV_ROWS = 32
 
@@ -233,7 +234,7 @@
 
     kv_step(jnp.int32(0))
 
-    for k in range(1, PLANE):
+    for k in FIRST_FAR:
         q_copy(k, q_ref, qg, q_ss, q_rs).start()
     my_cols = pl.ds(pl.multiple_of(core * 2 * HD, 2 * HD), 2 * HD)
     my_rows = pl.ds(pl.multiple_of(p * TOK, TOK), TOK)
@@ -266,10 +267,10 @@
         dst = plane_peer(k)
         return rcopy(etot.at[dst], ertot.at[p], et_ss.at[k], et_rs.at[k], {"ctx": base + dst})
 
-    for k in range(1, PLANE):
+    for k in FIRST_FAR:
         e_copy(k).start()
         et_copy(k).start()
-    for k in range(1, PLANE):
+    for k in FIRST_FAR:
         q_copy(k, do_ref, dog, do_ss, do_rs).start()
     erecv[p] = ebuf[p]
     ertot[p] = etot[p]
@@ -423,7 +424,7 @@
         dst = plane_peer(k)
         return rcopy(cbuf.at[dst], crecv.at[p], ec_ss.at[k], ec_rs.at[k], {"ctx": base + dst})
 
-    for k in range(1, PLANE):
+    for k in FIRST_FAR:
         c_copy(k).start()
     crecv[p] = cbuf[p]
 
@@ -497,7 +498,7 @@
                 s2[rows, cut] = a2
             return carry, h_now
 
-        lax.fori_loop(0, TOK // 8, backward, (g_in, h_end))
+        lax.fori_loop(0, TOK // 8, backward, (g_in, h_end), unroll=2)
         gxb[:, lanes] = (s1[...] * stf[:, lanes]).astype(BF16)
         gsb[:, lanes] = (
             s1[...] * xb[:, lanes].astype(F32) + LN2 * s2[...]
@@ -559,6 +560,29 @@
 
     dqt[...] = jnp.zeros_like(dqt)
 
+    def dq_to(dst):
+        cols = slice(dst * TOK, (dst + 1) * TOK)
+        return rcopy(
+            dqs.at[:, cols], dqr.at[p], dq_ss.at[dst], dq_rs.at[p], {"ctx": base + dst}
+        )
+
+    def dq_from(src):
+        return rcopy(
+            dqs.at[:, 0:TOK], dqr.at[src], dq_ss.at[src], dq_rs.at[src], {"ctx": base + src}
+        )
+
+    def dq_leave(first, last):
+        cols = slice(first * TOK, last * TOK)
+        dqs[:, cols] = (dqt[:, cols] * SCALE).astype(BF16)
+        for dst in range(first, last):
+            @pl.when(p != dst)
+            def _(dst=dst):
+                dq_to(dst).start()
+
+            @pl.when(p == dst)
+            def _(dst=dst):
+                dqr[dst] = dqs[:, dst * TOK:(dst + 1) * TOK]
+
     def attn_second(s, slot, diagonal):
         keys_t = kvg[slot, :, 0:HD].T
 
@@ -581,7 +605,16 @@
             return dk, dv
 
         zero = jnp.zeros((2 * TOK, HD), F32)
-        dk, dv = lax.fori_loop(0, 2 * 1024 // ROWS, body, (zero, zero), unroll=True)
+        if diagonal:
+            both = (zero, zero)
+            per_head = 1024 // ROWS
+            for part in range(per_head):
+                for head in range(2):
+                    both = body(jnp.int32(head * per_head + part), both)
+                dq_leave(part * PLANE // per_head, (part + 1) * PLANE // per_head)
+            dk, dv = both
+        else:
+            dk, dv = lax.fori_loop(0, 2 * 1024 // ROWS, body, (zero, zero), unroll=True)
         dk = dk * SCALE
         first = core == 0
         own[s, :, 0:HD] = jnp.where(first, dk[0:TOK], dk[TOK:])
@@ -618,6 +651,10 @@
             last = jnp.where(i == turn, n_chunks, 1)
             lax.fori_loop(first, last, second_chunk, 0)
 
+        @pl.when(jnp.logical_and(i > 0, i == turn))
+        def _():
+            hand_down(s + 1)
+
         @pl.when(i == turn)
         def _():
             coefficients()
@@ -634,7 +671,7 @@
         def _():
             attn_second(jnp.int32(0), z, True)
 
-        @pl.when(i > 0)
+        @pl.when(jnp.logical_and(i > 0, i != turn))
         def _():
             hand_down(s + 1)
 
@@ -646,26 +683,14 @@
 
     lax.fori_loop(0, z + 1, second_step, 0)
 
-    dqs[...] = (dqt[...] * SCALE).astype(BF16)
-
-    def dq_copy(k):
-        dst = plane_peer(k)
-        cols = pl.ds(pl.multiple_of(dst * TOK, TOK), TOK)
-        return rcopy(
-            dqs.at[:, cols], dqr.at[p], dq_ss.at[k], dq_rs.at[k], {"ctx": base + dst}
-        )
-
-    for k in range(1, PLANE):
-        dq_copy(k).start()
-    own_dq = pltpu.make_async_copy(
-        dqs.at[:, pl.ds(pl.multiple_of(p * TOK, TOK), TOK)], dqr.at[p], loc.at[4]
-    )
-    own_dq.start()
     sib_copy(jnp.int32(0)).wait()
 
-    for k in range(1, PLANE):
-        dq_copy(k).wait()
-    own_dq.wait()
+    for other in range(PLANE):
+        @pl.when(p != other)
+        def _(other=other):
+            dq_to(other).wait_send()
+            dq_from(other).wait_recv()
+
     for cc in range(2):
         tot = dqr[cc].astype(F32)
         for i in range(1, 4):

time: 80.8 us -> 78.5 us (0.972)
  Pallas kernels: 80 us -> 77.7 us
    pallas_call x1, Pallas kernels: 77.6 us -> 75.3 us  [on_device(): pl.pallas_call(kernel, out_shape=outs, in_specs=[pl.BlockSpec(memory_spac...]
where the time goes in v4:
time: 78.5 us; the launch traced here: 78.3 us
  Pallas kernels  77.7 us (99%)
    pallas_call x1, Pallas kernels, on_device(): pl.pallas_call(kernel, out_shape=outs, in_specs=[pl.BlockSpec(memory_spac...  75.3 us
    pallas_call x1, Pallas kernels, on_device(): pl.pallas_call(hand_over, out_shape=outs, in_specs=[pl.BlockSpec(memory_s...  2.39 us

profile of v4, /device:TPU:97, one launch (start us, length us, event | category | flops | bytes accessed | tf_op | source)
XLA Modules:
  0.0 78.3 jit_solution(16105913683963347993)
XLA Ops:
  0.6 75.3 %shard_map.153 = (bf16[128,512]{1,0:T(8,128)(2,1)}, bf16[128,128]{1,0:T(8,128)(2,1)}, bf16[128,128]{1,0:T(8,128)(2,1)}, bf16[128,2048]{1,0:T(8,128)(2,1)}, bf16[...) custom-call(bf16[128,512]{1,0:T(8,128)(2,1)} %q_ref.1, bf16[128,128]{1,0:T(8,128)(2,1)} %k_ref.1, ...), custom_call_target="tpu_custom_call" | custom-call | tf_op jit(solution)/shard_map/pallas_call | solution.py:806
  75.9 2.4 %shard_map.154 = (bf16[128,512]{1,0:T(8,128)(2,1)}, bf16[128,128]{1,0:T(8,128)(2,1)}, bf16[128,128]{1,0:T(8,128)(2,1)}, bf16[128,2048]{1,0:T(8,128)(2,1)}, bf16[...) custom-call(bf16[128,512]{1,0:T(8,128)(2,1)} %get-tuple-element.21.refs_0_, ...), custom_call_target="tpu_custom_call" | custom-call | tf_op jit(solution)/shard_map/pallas_call | solution.py:821
